TPU v7x, 512 devices: a whole 4x8x8 slice. The times are simulated.
512 devices in a mesh: seq: 128 (over x, y, z_lo, core), batch: 4 (over z_hi).
Axes of the slice: x: 4, y: 8, z: 8 (z_hi: 4, z_lo: 2; z = z_hi * 2 + z_lo), core: 2. Of those that a mesh axis runs over, the one named last changes fastest.
Arguments:
- queries: bfloat16 [65536, 1024], P(('batch', 'seq')), parts along dimension 0, may hold values from -150 to 150
- key_rows: bfloat16 [65536, 1024], P(('batch', 'seq')), parts along dimension 0, may hold values from -6 to 6
- value_rows: bfloat16 [65536, 1024], P(('batch', 'seq')), parts along dimension 0, may hold values from -6 to 6
- cotangent: bfloat16 [65536, 1024], P(('batch', 'seq')), parts along dimension 0, may hold values from -6 to 6
- matches: int32 [12, 128], P('batch'), parts along dimension 0, may hold values from 0 to 127, as said below
- active: int32 [12, 128], P('batch', 'seq'), parts along dimension 0, may hold values from 0 to 1, as said below
- global_pos: int32 [2048], P(('batch', 'seq')), parts along dimension 0, may hold values from 0 to 16383, as said below
Outputs:
- attended: bfloat16 [65536, 1024], P(('batch', 'seq')), parts along dimension 0
- query_grad: bfloat16 [65536, 1024], P(('batch', 'seq')), parts along dimension 0
- key_grad: bfloat16 [65536, 1024], P(('batch', 'seq')), parts along dimension 0
- value_grad: bfloat16 [65536, 1024], P(('batch', 'seq')), parts along dimension 0
There are 4 independent parts, one for each index of `batch`. A program takes and returns all parts, laid end to end along the dimension named above; each array names one. Nothing has to cross between parts.
Inputs may be any that keep to these rules, and one draw needn't show every extreme that they name: Each row r pairs the shards: matches[r, matches[r, s]] = s and matches[r, s] != s. Symmetric within each pair: active[r, s] = active[r, matches[r, s]]. `global_pos`: entries s * 4 to (s + 1) * 4 - 1 are increasing positions inside shard s.
All inputs are finite; a program needn't handle non-finite values.
Results may differ from a plain program's by a relative error of at most 0.018.
Values may be sent and summed in bfloat16 or wider, within the bound.
A program may use at most 64 MiB of HBM per device.

v0:
```python
import jax
import jax.numpy as jnp
from jax import lax
from jax.sharding import PartitionSpec as P

HEAD_DIM = 128
ROUNDS = 3


masked_score = -1e30


def route_pair(leading, trailing, partner_ids):
    shard_count = lax.axis_size("seq")
    tok_rows, feat_width = leading.shape
    lead_recv = lax.all_to_all(
        leading.reshape(shard_count, tok_rows // shard_count, feat_width),
        "seq",
        split_axis=0,
        concat_axis=0,
        tiled=True,
    )
    trail_recv = lax.all_to_all(
        trailing.reshape(shard_count, tok_rows // shard_count, feat_width),
        "seq",
        split_axis=0,
        concat_axis=0,
        tiled=True,
    )
    lead_moved = jnp.take(lead_recv, partner_ids, axis=0)
    trail_moved = jnp.take(trail_recv, partner_ids, axis=0)
    lead_out = lax.all_to_all(lead_moved, "seq", split_axis=0, concat_axis=0, tiled=True)
    trail_out = lax.all_to_all(trail_moved, "seq", split_axis=0, concat_axis=0, tiled=True)
    return (lead_out.reshape(tok_rows, feat_width), trail_out.reshape(tok_rows, feat_width))


def local(queries, key_rows, value_rows, cotangent, matches, active, global_pos):
    tok_rows, feat_width = queries.shape
    head_count = feat_width // HEAD_DIM
    shard_count = lax.axis_size("seq")
    position = lax.axis_index("seq")
    scaling = HEAD_DIM ** (-0.5)
    local_count = (ROUNDS + 1) * tok_rows
    local_pos = global_pos - position * tok_rows
    picker = (local_pos[:, None] == jnp.arange(tok_rows, dtype=jnp.int32)[None, :]).astype(
        jnp.bfloat16
    )
    picked_keys = jnp.dot(picker, key_rows, preferred_element_type=jnp.float32).astype(jnp.bfloat16)
    picked_values = jnp.dot(picker, value_rows, preferred_element_type=jnp.float32).astype(
        jnp.bfloat16
    )
    glob_keys, glob_values = (
        lax.all_gather(picked_keys, "seq", axis=0, tiled=True),
        lax.all_gather(picked_values, "seq", axis=0, tiled=True),
    )
    glob_count = glob_keys.shape[0]
    partner_keys = []
    partner_values = []
    for match_no in range(ROUNDS):
        got_keys, got_values = route_pair(key_rows, value_rows, matches[match_no])
        partner_keys.append(got_keys)
        partner_values.append(got_values)
    all_keys = jnp.concatenate([key_rows] + partner_keys + [glob_keys], axis=0).reshape(
        -1, head_count, HEAD_DIM
    )
    all_values = jnp.concatenate([value_rows] + partner_values + [glob_values], axis=0).reshape(
        -1, head_count, HEAD_DIM
    )
    keep = (
        jnp.concatenate(
            [
                jnp.ones((tok_rows,), jnp.int32),
                jnp.repeat(active[:, 0], tok_rows),
                jnp.ones((glob_count,), jnp.int32),
            ]
        )
        > 0
    )
    query_heads = queries.reshape(tok_rows, head_count, HEAD_DIM)
    grad_heads = cotangent.reshape(tok_rows, head_count, HEAD_DIM)

    def head_pass(items):
        query_one, key_one, value_one, grad_one = items
        scores = (
            jnp.einsum("qe,ke->qk", query_one, key_one, preferred_element_type=jnp.float32)
            * scaling
        )
        scores = jnp.where(keep[None, :], scores, masked_score)
        peak = jnp.max(scores, axis=1, keepdims=True)
        raw_weights = jnp.exp(scores - peak)
        probs = raw_weights / jnp.sum(raw_weights, axis=1, keepdims=True)
        probs_low = probs.astype(jnp.bfloat16)
        mixed = jnp.einsum("qk,ke->qe", probs_low, value_one, preferred_element_type=jnp.float32)
        grad_probs = jnp.einsum(
            "qe,ke->qk", grad_one, value_one, preferred_element_type=jnp.float32
        )
        centre = jnp.sum(grad_one.astype(jnp.float32) * mixed, axis=1)
        score_grad = (probs * (grad_probs - centre[:, None])).astype(jnp.bfloat16)
        query_grad = (
            jnp.einsum("qk,ke->qe", score_grad, key_one, preferred_element_type=jnp.float32)
            * scaling
        ).astype(jnp.bfloat16)
        grad_split = score_grad[:, :local_count].reshape(tok_rows, ROUNDS + 1, tok_rows)
        prob_split = probs_low[:, :local_count].reshape(tok_rows, ROUNDS + 1, tok_rows)
        key_part = (
            jnp.einsum("qrt,qe->tre", grad_split, query_one, preferred_element_type=jnp.float32)
            * scaling
        )
        value_part = jnp.einsum(
            "qrt,qe->tre", prob_split, grad_one, preferred_element_type=jnp.float32
        )
        return (
            mixed,
            query_grad,
            key_part,
            value_part,
            score_grad[:, local_count:],
            probs_low[:, local_count:],
        )

    head_items = (
        query_heads.transpose(1, 0, 2),
        all_keys.transpose(1, 0, 2),
        all_values.transpose(1, 0, 2),
        grad_heads.transpose(1, 0, 2),
    )
    mixed_h, query_grad_h, key_part_h, value_part_h, glob_grad, glob_prob = lax.map(
        head_pass, head_items
    )
    attended = mixed_h.astype(jnp.bfloat16).transpose(1, 0, 2).reshape(tok_rows, feat_width)
    query_grad = query_grad_h.transpose(1, 0, 2).reshape(tok_rows, feat_width)
    key_terms = key_part_h.transpose(1, 2, 0, 3).reshape(tok_rows, ROUNDS + 1, feat_width)
    value_terms = value_part_h.transpose(1, 2, 0, 3).reshape(tok_rows, ROUNDS + 1, feat_width)
    send_keys = key_terms[:, 1:].astype(jnp.bfloat16)
    send_values = value_terms[:, 1:].astype(jnp.bfloat16)
    key_total = key_terms[:, 0]
    value_total = value_terms[:, 0]
    for match_no in range(ROUNDS):
        back_keys, back_values = route_pair(
            send_keys[:, match_no], send_values[:, match_no], matches[match_no]
        )
        key_total = key_total + back_keys.astype(jnp.float32)
        value_total = value_total + back_values.astype(jnp.float32)
    own_glob = glob_count // shard_count
    key_glob = (
        jnp.einsum("hqk,qhe->khe", glob_grad, query_heads, preferred_element_type=jnp.float32)
        * scaling
    )
    value_glob = jnp.einsum(
        "hqk,qhe->khe", glob_prob, grad_heads, preferred_element_type=jnp.float32
    )
    summed = lax.psum(
        jnp.concatenate(
            [key_glob.reshape(glob_count, feat_width), value_glob.reshape(glob_count, feat_width)],
            axis=1,
        ),
        "seq",
    )
    mine = lax.dynamic_slice_in_dim(summed, position * own_glob, own_glob, 0)
    key_total = key_total.at[local_pos].add(mine[:, :feat_width])
    value_total = value_total.at[local_pos].add(mine[:, feat_width:])
    return (attended, query_grad, key_total.astype(jnp.bfloat16), value_total.astype(jnp.bfloat16))


def solution(mesh):
    return jax.shard_map(
        local,
        mesh=mesh,
        in_specs=(
            P(("batch", "seq"), None),
            P(("batch", "seq"), None),
            P(("batch", "seq"), None),
            P(("batch", "seq"), None),
            P("batch", None),
            P("batch", "seq"),
            P(("batch", "seq")),
        ),
        out_specs=(
            P(("batch", "seq"), None),
            P(("batch", "seq"), None),
            P(("batch", "seq"), None),
            P(("batch", "seq"), None),
        ),
        check_vma=False,
    )
```

profile of v0, /device:TPU:1, one launch (start us, length us, event | category | flops | bytes accessed | tf_op | source)
XLA Modules:
  0.0 1817.7 jit_solution(13352272256983482966)
XLA Ops:
  10.4 14.2 all-to-all-start
  27.3 11.6 all-to-all-done
  38.9 5.5 all-to-all-start.4
  44.8 14.0 all-to-all-done.4
  62.7 5.5 all-to-all-start.1
  72.7 9.9 all-to-all-done.1
  82.6 6.1 all-to-all-start.2
  92.2 11.1 all-to-all-done.2
  103.4 5.4 all-to-all-start.3
  110.5 13.0 all-to-all-done.3
  123.4 5.5 all-to-all-start.5
  130.7 12.9 all-to-all-done.5
  143.6 5.4 all-to-all-start.6
  154.7 9.0 all-to-all-done.6
  163.7 6.8 all-to-all-start.7
  193.5 94.1 %all-gather.5.cloned.1.call-done = bf16[128,4,1024]{2,1,0:T(4,128)(2,1)} async-done(((bf16[1,4,1024]{2,1,0:T(4,128)(2,1)}), bf16[128,4,1024]{2,1,0:T(4,128)(2,1)}) %all-gather.5.cloned.1.call-update) | async-done | bytes 1048592 | tf_op jit(solution)/shard_map/all_gather | solution.py:53
  289.4 211.8 %all-gather.7.cloned.1.call-done = bf16[128,4,1024]{2,1,0:T(4,128)(2,1)} async-done(((bf16[1,4,1024]{2,1,0:T(4,128)(2,1)}), bf16[128,4,1024]{2,1,0:T(4,128)(2,1)}) %all-gather.7.cloned.1.call-update) | async-done | bytes 1048592 | tf_op jit(solution)/shard_map/all_gather | solution.py:54
  503.8 69.9 %while.20 = (s32[]{:T(128)}, bf16[8,128,128]{1,2,0:T(8,128)(2,1)}, bf16[8,128,128]{2,1,0:T(8,128)(2,1)}, f32[8,128,4,128]{1,3,2,0:T(8,128)}, f32[8,128,4,128]{1,...) while((s32[]{:T(128)}, bf16[8,128,128]{1,2,0:T(8,128)(2,1)}, ...), condition=%wide.region_4.6_spmd, body=%wide.region_0.5_spmd.sunk | while | flops 169623168 | bytes 5910657 | solution.py:127
  573.7 3.1 copy.117
  579.3 2.4 fusion.55
  581.6 2.3 reduce.15
  584.8 13.2 all-to-all-start.8
  598.0 3.1 copy.123
  601.2 2.9 reshape.138
  606.2 2.3 fusion.54
  608.5 3.2 reduce.14
  612.6 12.8 all-to-all-start.14
  625.3 3.9 reduce.10
  631.1 8.1 all-to-all-done.14
  639.2 6.5 all-to-all-start.10
  645.7 3.9 reduce.9
  651.4 8.3 all-to-all-done.10
  659.8 6.9 all-to-all-start.12
  666.7 3.9 reduce.11
  672.4 3.0 convolution_multiply_fusion.3
  675.4 2.9 copy.121
  678.3 2.4 all-to-all-done.12
  680.7 10.0 all-to-all-start.16
  690.8 3.0 fusion.56
  693.7 2.9 copy.122
  696.6 4.7 pad_maximum_fusion
  701.4 2.3 reduce.8
  705.0 12.1 all-to-all-start.18
  724.0 7.6 all-to-all-done.18
  731.6 5.4 all-to-all-start.15
  736.9 2.2 reshape.370
  740.8 2.2 reshape.366
  752.6 12.4 all-to-all-start.19
  767.7 11.9 all-to-all-done.19
  779.6 5.3 all-to-all-start.17
  786.6 12.9 all-to-all-done.17
  799.5 5.7 all-to-all-start.9
  807.9 12.3 all-to-all-done.9
  820.1 5.3 all-to-all-start.11
  825.5 2.4 reduce.12
  829.8 10.7 all-to-all-done.11
  840.4 6.5 all-to-all-start.13
  851.0 2.9 reshape.384
  853.8 3.4 fusion.44
  858.4 2.2 reshape.372
  860.8 2.8 reshape.368
  863.7 2.7 fusion.46
  866.4 938.1 %all-reduce.2.cloned.1.call-done = f32[512,2048]{1,0:T(8,128)} async-done(((f32[512,2048]{1,0:T(8,128)}), f32[512,2048]{1,0:T(8,128)}) %all-reduce.2.cloned.1.call-update) | async-done | bytes 4194320 | tf_op jit(solution)/shard_map/psum | solution.py:152
  1804.5 2.7 scatter_custom_fusion.1
  (282 shorter events, 173.4 us)
Async XLA Ops:
  7.2 163.3 %copy-start = (s32[3,1]{0,1:T(1,128)S(1)}, s32[3,1]{0,1:T(1,128)}, u32[]{:S(2)}) copy-start(s32[3,1]{0,1:T(1,128)} %param.16) | copy-start | bytes 40
  7.2 37.2 %copy-start.28 = (s32[3,128]{1,0:T(4,128)S(1)}, s32[3,128]{1,0:T(4,128)}, u32[]{:S(2)}) copy-start(s32[3,128]{1,0:T(4,128)} %param.15) | copy-start | bytes 4612
  10.4 28.5 %all-to-all-start = ((bf16[128,2,512]{2,1,0:T(2,128)(2,1)}), bf16[128,2,512]{2,1,0:T(2,128)(2,1)S(1)}, u32[]{:S(2)}, u32[]{:S(2)}) async-start(bf16[128,2,512]{2,1,0:T(2,128)(2,1)} %reshape.349), calls=%async_computation | async-start | bytes 524288 | tf_op jit(solution)/shard_map/all_to_all | solution.py:16
  38.9 19.9 %all-to-all-start.4 = ((bf16[128,2,512]{2,1,0:T(2,128)(2,1)}), bf16[128,2,512]{2,1,0:T(2,128)(2,1)S(1)}, u32[]{:S(2)}, u32[]{:S(2)}) async-start(bf16[128,2,512]{2,1,0:T(2,128)(2,1)} %reshape.357), calls=%async_computation.4 | async-start | bytes 524288 | tf_op jit(solution)/shard_map/all_to_all | solution.py:23
  60.0 8.3 copy-start.29
  60.0 8.3 copy-start.17
  62.7 19.9 %all-to-all-start.1 = ((bf16[128,2,512]{2,1,0:T(2,128)(2,1)}), bf16[128,2,512]{2,1,0:T(2,128)(2,1)S(1)}, u32[]{:S(2)}, u32[]{:S(2)}) async-start(bf16[128,2,512]{2,1,0:T(2,128)(2,1)} %reshape.351), calls=%async_computation.1 | async-start | bytes 524288 | tf_op jit(solution)/shard_map/all_to_all | solution.py:32
  68.2 219.4 %all-gather.5.cloned.1.call-start = ((), (), s32[]{:S(2)}) async-start(), calls=%async_computation.21 | async-start | bytes 1056768 | tf_op jit(solution)/shard_map/all_gather | solution.py:53
  82.6 20.8 %all-to-all-start.2 = ((bf16[128,2,512]{2,1,0:T(2,128)(2,1)}), bf16[128,2,512]{2,1,0:T(2,128)(2,1)S(1)}, u32[]{:S(2)}, u32[]{:S(2)}) async-start(bf16[128,2,512]{2,1,0:T(2,128)(2,1)} %reshape.353), calls=%async_computation.2 | async-start | bytes 524288 | tf_op jit(solution)/shard_map/all_to_all | solution.py:32
  91.3 57.7 %copy-start.18 = (bf16[128,1024]{1,0:T(8,128)(2,1)S(1)}, bf16[128,1024]{1,0:T(8,128)(2,1)}, u32[]{:S(2)}) copy-start(bf16[128,1024]{1,0:T(8,128)(2,1)} %param.13) | copy-start | bytes 786436
  103.4 20.1 %all-to-all-start.3 = ((bf16[128,2,512]{2,1,0:T(2,128)(2,1)}), bf16[128,2,512]{2,1,0:T(2,128)(2,1)S(1)}, u32[]{:S(2)}, u32[]{:S(2)}) async-start(bf16[128,2,512]{2,1,0:T(2,128)(2,1)} %reshape.355), calls=%async_computation.3 | async-start | bytes 524288 | tf_op jit(solution)/shard_map/all_to_all | solution.py:32
  123.4 28.6 %copy-start.3 = (bf16[128,2,512]{2,1,0:T(2,128)(2,1)}, bf16[128,2,512]{2,1,0:T(2,128)(2,1)S(1)}, u32[]{:S(2)}) copy-start(bf16[128,2,512]{2,1,0:T(2,128)(2,1)S(1)} %all-to-all-done.3) | copy-start | bytes 786436
  123.4 20.2 %all-to-all-start.5 = ((bf16[128,2,512]{2,1,0:T(2,128)(2,1)}), bf16[128,2,512]{2,1,0:T(2,128)(2,1)S(1)}, u32[]{:S(2)}, u32[]{:S(2)}) async-start(bf16[128,2,512]{2,1,0:T(2,128)(2,1)} %reshape.359), calls=%async_computation.5 | async-start | bytes 524288 | tf_op jit(solution)/shard_map/all_to_all | solution.py:33
  128.9 23.1 %copy-start.26 = (bf16[128,1024]{1,0:T(8,128)(2,1)S(1)}, bf16[128,1024]{1,0:T(8,128)(2,1)}, u32[]{:S(2)}) copy-start(bf16[128,1024]{1,0:T(8,128)(2,1)} %param.11) | copy-start | bytes 786436
  129.8 23.1 %copy-start.27 = (bf16[128,1024]{1,0:T(8,128)(2,1)S(1)}, bf16[128,1024]{1,0:T(8,128)(2,1)}, u32[]{:S(2)}) copy-start(bf16[128,1024]{1,0:T(8,128)(2,1)} %param.14) | copy-start | bytes 786436
  143.6 10.2 copy-start.5
  143.6 20.1 %all-to-all-start.6 = ((bf16[128,2,512]{2,1,0:T(2,128)(2,1)}), bf16[128,2,512]{2,1,0:T(2,128)(2,1)S(1)}, u32[]{:S(2)}, u32[]{:S(2)}) async-start(bf16[128,2,512]{2,1,0:T(2,128)(2,1)} %reshape.361), calls=%async_computation.6 | async-start | bytes 524288 | tf_op jit(solution)/shard_map/all_to_all | solution.py:33
  149.0 352.1 %all-gather.7.cloned.1.call-start = ((), (), s32[]{:S(2)}) async-start(), calls=%async_computation.22 | async-start | bytes 1056768 | tf_op jit(solution)/shard_map/all_gather | solution.py:54
  163.7 6.9 copy-start.9
  163.7 21.9 %all-to-all-start.7 = ((bf16[128,2,512]{2,1,0:T(2,128)(2,1)}), bf16[128,2,512]{2,1,0:T(2,128)(2,1)}, u32[]{:S(2)}, u32[]{:S(2)}) async-start(bf16[128,2,512]{2,1,0:T(2,128)(2,1)} %reshape.363), calls=%async_computation.7 | async-start | bytes 524288 | tf_op jit(solution)/shard_map/all_to_all | solution.py:33
  173.5 5.9 copy-start.4
  176.6 6.0 copy-start.6
  179.7 4.4 copy-start.10
  184.1 5.1 copy-start.19
  188.3 3.0 copy-start.20
  188.3 3.7 copy-start.21
  189.2 3.6 copy-start.22
  584.8 27.7 %all-to-all-start.8 = ((bf16[128,2,512]{2,1,0:T(2,128)(2,1)}), bf16[128,2,512]{2,1,0:T(2,128)(2,1)S(1)}, u32[]{:S(2)}, u32[]{:S(2)}) async-start(bf16[128,2,512]{2,1,0:T(2,128)(2,1)} %reshape.373), calls=%async_computation.8 | async-start | bytes 524288 | tf_op jit(solution)/shard_map/all_to_all | solution.py:16
  612.6 26.6 %all-to-all-start.14 = ((bf16[128,2,512]{2,1,0:T(2,128)(2,1)}), bf16[128,2,512]{2,1,0:T(2,128)(2,1)}, u32[]{:S(2)}, u32[]{:S(2)}) async-start(bf16[128,2,512]{2,1,0:T(2,128)(2,1)} %reshape.385), calls=%async_computation.14 | async-start | bytes 524288 | tf_op jit(solution)/shard_map/all_to_all | solution.py:23
  629.2 43.2 %copy-start.2 = (bf16[8,128,128]{1,2,0:T(8,128)(2,1)S(1)}, bf16[8,128,128]{1,2,0:T(8,128)(2,1)}, u32[]{:S(2)}) copy-start(bf16[8,128,128]{1,2,0:T(8,128)(2,1)} %get-tuple-element.270) | copy-start | bytes 786436
  639.2 20.6 %all-to-all-start.10 = ((bf16[128,2,512]{2,1,0:T(2,128)(2,1)}), bf16[128,2,512]{2,1,0:T(2,128)(2,1)}, u32[]{:S(2)}, u32[]{:S(2)}) async-start(bf16[128,2,512]{2,1,0:T(2,128)(2,1)} %reshape.369), calls=%async_computation.10 | async-start | bytes 524288 | tf_op jit(solution)/shard_map/all_to_all | solution.py:16
  659.8 21.0 %all-to-all-start.12 = ((bf16[128,2,512]{2,1,0:T(2,128)(2,1)}), bf16[128,2,512]{2,1,0:T(2,128)(2,1)}, u32[]{:S(2)}, u32[]{:S(2)}) async-start(bf16[128,2,512]{2,1,0:T(2,128)(2,1)} %reshape.365), calls=%async_computation.12 | async-start | bytes 524288 | tf_op jit(solution)/shard_map/all_to_all | solution.py:16
  680.7 24.2 %all-to-all-start.16 = ((bf16[128,2,512]{2,1,0:T(2,128)(2,1)}), bf16[128,2,512]{2,1,0:T(2,128)(2,1)S(1)}, u32[]{:S(2)}, u32[]{:S(2)}) async-start(bf16[128,2,512]{2,1,0:T(2,128)(2,1)} %reshape.381), calls=%async_computation.16 | async-start | bytes 524288 | tf_op jit(solution)/shard_map/all_to_all | solution.py:23
  690.7 1113.8 %all-reduce.2.cloned.1.call-start = ((), (), s32[]{:S(2)}) async-start(), calls=%async_computation.20 | async-start | bytes 8388608 | tf_op jit(solution)/shard_map/psum | solution.py:152
  705.0 12.2 copy-start.7
  705.0 26.6 %all-to-all-start.18 = ((bf16[128,2,512]{2,1,0:T(2,128)(2,1)}), bf16[128,2,512]{2,1,0:T(2,128)(2,1)S(1)}, u32[]{:S(2)}, u32[]{:S(2)}) async-start(bf16[128,2,512]{2,1,0:T(2,128)(2,1)} %reshape.377), calls=%async_computation.18 | async-start | bytes 524288 | tf_op jit(solution)/shard_map/all_to_all | solution.py:23
  731.6 7.6 copy-start.14
  731.6 21.1 %all-to-all-start.15 = ((bf16[128,2,512]{2,1,0:T(2,128)(2,1)}), bf16[128,2,512]{2,1,0:T(2,128)(2,1)S(1)}, u32[]{:S(2)}, u32[]{:S(2)}) async-start(bf16[128,2,512]{2,1,0:T(2,128)(2,1)} %reshape.387), calls=%async_computation.15 | async-start | bytes 524288 | tf_op jit(solution)/shard_map/all_to_all | solution.py:33
  740.8 3.9 copy-start.8
  744.9 1.7 copy-start.15
  746.8 1.0 copy-start.24
  746.9 1.0 copy-start.25
  749.9 35.0 %copy-start.23 = (bf16[128,1,1024]{2,0,1:T(8,128)(2,1)S(1)}, bf16[128,1,1024]{2,0,1:T(8,128)(2,1)}, u32[]{:S(2)}) copy-start(bf16[128,1,1024]{2,0,1:T(8,128)(2,1)} %get-tuple-element.127) | copy-start | bytes 786436
  752.6 27.0 %all-to-all-start.19 = ((bf16[128,2,512]{2,1,0:T(2,128)(2,1)}), bf16[128,2,512]{2,1,0:T(2,128)(2,1)S(1)}, u32[]{:S(2)}, u32[]{:S(2)}) async-start(bf16[128,2,512]{2,1,0:T(2,128)(2,1)} %reshape.379), calls=%async_computation.19 | async-start | bytes 524288 | tf_op jit(solution)/shard_map/all_to_all | solution.py:33
  779.6 19.9 %all-to-all-start.17 = ((bf16[128,2,512]{2,1,0:T(2,128)(2,1)}), bf16[128,2,512]{2,1,0:T(2,128)(2,1)S(1)}, u32[]{:S(2)}, u32[]{:S(2)}) async-start(bf16[128,2,512]{2,1,0:T(2,128)(2,1)} %reshape.383), calls=%async_computation.17 | async-start | bytes 524288 | tf_op jit(solution)/shard_map/all_to_all | solution.py:33
  799.5 49.2 %copy-start.11 = (bf16[128,2,512]{2,1,0:T(2,128)(2,1)}, bf16[128,2,512]{2,1,0:T(2,128)(2,1)S(1)}, u32[]{:S(2)}) copy-start(bf16[128,2,512]{2,1,0:T(2,128)(2,1)S(1)} %all-to-all-done.17) | copy-start | bytes 786436
  799.5 20.6 %all-to-all-start.9 = ((bf16[128,2,512]{2,1,0:T(2,128)(2,1)}), bf16[128,2,512]{2,1,0:T(2,128)(2,1)S(1)}, u32[]{:S(2)}, u32[]{:S(2)}) async-start(bf16[128,2,512]{2,1,0:T(2,128)(2,1)} %reshape.375), calls=%async_computation.9 | async-start | bytes 524288 | tf_op jit(solution)/shard_map/all_to_all | solution.py:32
  820.1 28.5 %copy-start.12 = (bf16[128,2,512]{2,1,0:T(2,128)(2,1)}, bf16[128,2,512]{2,1,0:T(2,128)(2,1)S(1)}, u32[]{:S(2)}) copy-start(bf16[128,2,512]{2,1,0:T(2,128)(2,1)S(1)} %all-to-all-done.9) | copy-start | bytes 786436
  820.1 20.3 %all-to-all-start.11 = ((bf16[128,2,512]{2,1,0:T(2,128)(2,1)}), bf16[128,2,512]{2,1,0:T(2,128)(2,1)S(1)}, u32[]{:S(2)}, u32[]{:S(2)}) async-start(bf16[128,2,512]{2,1,0:T(2,128)(2,1)} %reshape.371), calls=%async_computation.11 | async-start | bytes 524288 | tf_op jit(solution)/shard_map/all_to_all | solution.py:32
  840.4 10.0 copy-start.16
  840.4 20.4 %all-to-all-start.13 = ((bf16[128,2,512]{2,1,0:T(2,128)(2,1)}), bf16[128,2,512]{2,1,0:T(2,128)(2,1)}, u32[]{:S(2)}, u32[]{:S(2)}) async-start(bf16[128,2,512]{2,1,0:T(2,128)(2,1)} %reshape.367), calls=%async_computation.13 | async-start | bytes 524288 | tf_op jit(solution)/shard_map/all_to_all | solution.py:32
  850.9 7.2 copy-start.13
  863.7 947.2 %copy-start.1 = (s32[3,1]{0,1:T(1,128)S(1)}, s32[3,1]{0,1:T(1,128)}, u32[]{:S(2)}) copy-start(s32[3,1]{0,1:T(1,128)} %param.16) | copy-start | bytes 40
Sparse Core Ops, SparseCore 0:
  71.2 216.4 all-gather.4
  289.8 211.2 all-gather.6
  701.5 1102.9 all-reduce.1
where the time goes:
time: 1830 us; the launch traced here: 1820 us
  waiting for transfers between devices  1400 us (77%)
  starting transfers between devices  157 us (9%)
  local copies, waits for them, and re-layouts  114 us (6%)
  matrix products  67.8 us (4%)
  other arithmetic  63.8 us (3%)
    psum x1, waiting for transfers between devices, local(): lax.psum(jnp.concatenate([key_glob.reshape(glob_count, feat_width), value...  938 us
    all_gather x1, waiting for transfers between devices, local(): lax.all_gather(picked_values, 'seq', axis=0, tiled=True)  212 us
    all_gather x1, waiting for transfers between devices, local(): lax.all_gather(picked_keys, 'seq', axis=0, tiled=True)  94.1 us
    all_to_all x6, waiting for transfers between devices, route_pair(): lax.all_to_all(lead_moved, 'seq', split_axis=0, concat_axis=0, tiled=True)  57.3 us
    unnamed x122, local copies, waits for them, and re-layouts  51.3 us
    all_to_all x6, waiting for transfers between devices, route_pair(): lax.all_to_all(trail_moved, 'seq', split_axis=0, concat_axis=0, tiled=True)  46.7 us
    all_to_all x4, starting transfers between devices, route_pair(): lax.all_to_all(leading.reshape(shard_count, tok_rows // shard_count, feat...  40.9 us
    all_to_all x6, starting transfers between devices, route_pair(): lax.all_to_all(trail_moved, 'seq', split_axis=0, concat_axis=0, tiled=True)  40.7 us
  transfers between devices with their start and end apart: 23, of which 20 were waited for; matrix products, arithmetic and copies ran while one was open for 8% of the time, Pallas kernels for 0%

commit v1 on v0

v1 whole, which is shorter than its diff:
```python
import jax
import jax.numpy as jnp
from jax import lax
from jax.experimental import pallas as pl
from jax.experimental.pallas import tpu as pltpu
from jax.sharding import PartitionSpec as P

HD = 128
ROUNDS = 3
NY = 8
NP = 16
TOK = 128
SCALE = HD**-0.5
LOG2E = 1.4426950408889634
BF = jnp.bfloat16
F32 = jnp.float32


def mm(a, b):
    return lax.dot_general(a, b, (((1,), (0,)), ((), ())), preferred_element_type=F32)


def mm_t(a, b):
    return lax.dot_general(a, b, (((1,), (1,)), ((), ())), preferred_element_type=F32)


def kernel(
    matches, active, gpos, q_in, k_in, v_in, g_in,
    o_out, dq_out, dk_out, dv_out,
    aux, aux_all, kv, qg, inter, stage, part, gl_mine, gl_all,
    k_all, v_all, ret_stage, ret, tot_stage, tot, own, gacc, gg_stage, gg,
    od_stage, kvg_stage,
    sem_aux, sem_kv, sem_qg, sem_inter, sem_part, sem_gl, sem_ret, sem_tot, sem_gg, sem_out,
    send_aux, send_kv, send_qg, send_inter, send_part, send_gl, send_ret, send_tot, send_gg, send_od, send_kvg,
):
    me = lax.axis_index("seq")
    my_x, my_y, my_zc = me // 32, (me // 4) % NY, me % 4
    my_p = my_x * 4 + my_zc

    def line(y):
        return {"seq": my_x * 32 + y * 4 + my_zc}

    def plane(p):
        return {"seq": (p // 4) * 32 + my_y * 4 + p % 4}

    def put(src, dst, send, recv, where):
        pltpu.make_async_remote_copy(
            src_ref=src, dst_ref=dst, send_sem=send, recv_sem=recv, device_id=where,
            device_id_type=pl.DeviceIdType.MESH,
        ).start()

    def keep(src, dst, recv):
        pltpu.make_async_copy(src, dst, recv).start()

    def wait(ref, sem):
        pltpu.make_async_copy(ref, ref, sem).wait()

    def cols(ref, y):
        return ref.at[:, pl.ds(pl.multiple_of(y * HD, HD), HD)]

    barrier = pltpu.get_barrier_semaphore()

    @pl.loop(1, NY)
    def _(n):
        pl.semaphore_signal(barrier, inc=1, device_id=line((my_y + n) % NY), device_id_type=pl.DeviceIdType.MESH)

    @pl.loop(1, NP)
    def _(n):
        pl.semaphore_signal(barrier, inc=1, device_id=plane((my_p + n) % NP), device_id_type=pl.DeviceIdType.MESH)

    row = lax.broadcasted_iota(jnp.int32, (32, TOK), 0)
    lane = lax.broadcasted_iota(jnp.int32, (32, TOK), 1)
    tile = jnp.zeros((32, TOK), F32)
    for n in range(4):
        here = (row == (my_y % 4) * 4 + n) & (lane == gpos[n] - me * TOK)
        tile = jnp.where(here, 1.0, tile)
    for r in range(ROUNDS):
        tile = jnp.where(row == 16 + r, active[r, 0].astype(F32), tile)
    aux[...] = tile.astype(BF)

    pl.semaphore_wait(barrier, NY - 1 + NP - 1)

    keep(aux, aux_all.at[my_y], sem_aux)
    keep(cols(k_in, my_y), kv.at[0, my_y], sem_kv)
    keep(cols(v_in, my_y), kv.at[1, my_y], sem_kv)
    keep(cols(q_in, my_y), qg.at[0, my_y], sem_qg)
    keep(cols(g_in, my_y), qg.at[1, my_y], sem_qg)

    @pl.loop(1, NY)
    def _(n):
        y = (my_y + n) % NY
        put(aux, aux_all.at[my_y], send_aux, sem_aux, line(y))
        put(cols(k_in, y), kv.at[0, my_y], send_kv, sem_kv, line(y))
        put(cols(v_in, y), kv.at[1, my_y], send_kv, sem_kv, line(y))

    @pl.loop(1, NY)
    def _(n):
        y = (my_y + n) % NY
        put(cols(q_in, y), qg.at[0, my_y], send_qg, sem_qg, line(y))
        put(cols(g_in, y), qg.at[1, my_y], send_qg, sem_qg, line(y))

    wait(kv, sem_kv)

    def tile_of(p):
        return kv.at[p % 2, :, pl.ds(pl.multiple_of((p // 2) * 16, 16), 16), :]

    keep(tile_of(my_p), inter.at[my_x, :, my_zc], sem_inter)

    @pl.loop(1, NP)
    def _(n):
        p = (my_p + n) % NP
        put(tile_of(p), inter.at[my_x, :, my_zc], send_inter, sem_inter, plane(p))

    wait(aux_all, sem_aux)
    for half in range(2):
        picks = jnp.concatenate([aux_all[half * 4 + n, :16] for n in range(4)], axis=1)
        for which in range(2):
            rows = kv[which, half * 4 : half * 4 + 4].reshape(4 * TOK, HD)
            gl_mine[which, half * 16 : half * 16 + 16] = mm(picks, rows).astype(BF)
    keep(gl_mine, gl_all.at[my_p], sem_gl)

    @pl.loop(1, NP)
    def _(n):
        put(gl_mine, gl_all.at[my_p], send_gl, sem_gl, plane((my_p + n) % NP))

    wait(inter, sem_inter)

    def pick(p):
        for t in range(NY):
            s = (p // 4) * 32 + t * 4 + p % 4
            for r in range(ROUNDS):
                m = matches[r, s]
                stage[p, t, r] = inter[m // 32, (m // 4) % NY, m % 4]

    @pl.loop(1, NP)
    def _(n):
        p = (my_p + n) % NP
        pick(p)
        put(stage.at[p], part.at[my_p // 2, my_p % 2], send_part, sem_part, plane(p))

    pick(my_p)
    keep(stage.at[my_p], part.at[my_p // 2, my_p % 2], sem_part)

    wait(gl_all, sem_gl)
    k_all[512:] = gl_all[:, 0].reshape(512, HD)
    v_all[512:] = gl_all[:, 1].reshape(512, HD)
    gacc[...] = jnp.zeros_like(gacc)
    wait(qg, sem_qg)
    wait(part, sem_part)

    @pl.loop(0, NY)
    def _(n):
        t = (my_y + n) % NY
        q, g = qg[0, t], qg[1, t]
        k_all[0:TOK] = kv[0, t]
        v_all[0:TOK] = kv[1, t]
        for r in range(ROUNDS):
            k_all[TOK * (r + 1) : TOK * (r + 2)] = part[:, 0, t, r].reshape(TOK, HD)
            v_all[TOK * (r + 1) : TOK * (r + 2)] = part[:, 1, t, r].reshape(TOK, HD)
        keys, values = k_all[...], v_all[...]
        flags = [aux_all[t, 16:32].astype(F32)[r : r + 1] for r in range(ROUNDS)]
        bias = jnp.concatenate(
            [jnp.zeros((1, TOK), F32)] + [(f - 1.0) * 1e30 for f in flags] + [jnp.zeros((1, 512), F32)], axis=1
        )
        scores = mm_t(q, keys) * (SCALE * LOG2E) + bias
        weights = jnp.exp2(scores - jnp.max(scores, axis=1, keepdims=True))
        probs = weights * (1.0 / jnp.sum(weights, axis=1, keepdims=True))
        low = probs.astype(BF)
        gp = mm_t(g, values)
        centre = jnp.sum(low.astype(F32) * gp, axis=1, keepdims=True)
        sg = (probs * (gp - centre)).astype(BF)
        od_stage[0, t] = mm(low, values).astype(BF)
        od_stage[1, t] = (mm(sg, keys) * SCALE).astype(BF)

        @pl.when(n == 0)
        def _():
            keep(od_stage.at[0, t], cols(o_out, my_y), sem_out.at[0])
            keep(od_stage.at[1, t], cols(dq_out, my_y), sem_out.at[1])

        @pl.when(n > 0)
        def _():
            put(od_stage.at[0, t], cols(o_out, my_y), send_od, sem_out.at[0], line(t))
            put(od_stage.at[1, t], cols(dq_out, my_y), send_od, sem_out.at[1], line(t))

        kt = mm(q.T, sg) * SCALE
        vt = mm(g.T, low)
        for which, term in ((0, kt), (1, vt)):
            own[which, t] = term[:, :TOK]
            for r in range(ROUNDS):
                ret_stage[:, which, t, r] = term[:, TOK * (r + 1) : TOK * (r + 2)].astype(BF).reshape(8, 16, TOK)
            gacc[which] += term[:, 512:]

        keep(ret_stage.at[my_p // 2, my_p % 2, t], ret.at[my_x, t, my_zc], sem_ret)

        @pl.loop(1, NP)
        def _(i):
            p = (my_p + i) % NP
            put(ret_stage.at[p // 2, p % 2, t], ret.at[my_x, t, my_zc], send_ret, sem_ret, plane(p))

    for which in range(2):
        gg_stage[:, which] = gacc[which].T.astype(BF).reshape(NP, 32, HD)
    keep(gg_stage.at[my_p], gg.at[my_p], sem_gg)

    @pl.loop(1, NP)
    def _(n):
        p = (my_p + n) % NP
        put(gg_stage.at[p], gg.at[my_p], send_gg, sem_gg, plane(p))

    wait(ret, sem_ret)

    def total(p):
        for t in range(NY):
            s = (p // 4) * 32 + t * 4 + p % 4
            terms = []
            for r in range(ROUNDS):
                m = matches[r, s]
                terms.append(ret[m // 32, (m // 4) % NY, m % 4, r].astype(F32))
            tot_stage[p, t] = (terms[0] + terms[1] + terms[2]).astype(BF)

    @pl.loop(1, NP)
    def _(n):
        p = (my_p + n) % NP
        total(p)
        put(tot_stage.at[p], tot.at[my_p // 2, my_p % 2], send_tot, sem_tot, plane(p))

    total(my_p)
    keep(tot_stage.at[my_p], tot.at[my_p // 2, my_p % 2], sem_tot)

    wait(gg, sem_gg)
    gsum = [jnp.sum(gg[:, which].astype(F32), axis=0) for which in range(2)]
    for which in range(2):
        gacc[which, :32, :HD] = gsum[which]
    wait(tot, sem_tot)

    @pl.loop(0, NY)
    def _(n):
        t = (my_y + n) % NY
        spots = aux_all[t, :16]
        for which, out in ((0, dk_out), (1, dv_out)):
            rows = gacc[which, pl.ds(pl.multiple_of((t // 4) * 16, 16), 16), :HD].astype(BF)
            back = own[which, t] + tot[:, which, t].reshape(HD, TOK).astype(F32)
            there = lax.dot_general(spots, rows, (((0,), (0,)), ((), ())), preferred_element_type=F32)
            kvg_stage[which, t] = (back.T + there).astype(BF)

            @pl.when(n == 0)
            def _():
                keep(kvg_stage.at[which, t], cols(out, my_y), sem_out.at[2 + which])

            @pl.when(n > 0)
            def _():
                put(kvg_stage.at[which, t], cols(out, my_y), send_kvg, sem_out.at[2 + which], line(t))

    wait(o_out, sem_out.at[0])
    wait(dq_out, sem_out.at[1])
    wait(dk_out, sem_out.at[2])
    wait(dv_out, sem_out.at[3])
    wait(aux_all.at[: NY - 1], send_aux)
    for sem in (send_kv, send_qg, send_od, send_kvg):
        wait(kv.at[:, : NY - 1], sem)
    for sem in (send_inter, send_tot):
        wait(tot_stage.at[: NP - 1], sem)
    for sem in (send_part, send_ret):
        wait(stage.at[: NP - 1], sem)
    for sem in (send_gl, send_gg):
        wait(gg_stage.at[: NP - 1], sem)


def local(queries, key_rows, value_rows, cotangent, matches, active, global_pos):
    out = jax.ShapeDtypeStruct(queries.shape, BF)
    smem, vmem, hbm = (pl.BlockSpec(memory_space=m) for m in (pltpu.SMEM, pltpu.VMEM, pl.ANY))
    dma = pltpu.SemaphoreType.DMA
    return pl.pallas_call(
        kernel,
        out_shape=(out,) * 4,
        in_specs=[smem] * 3 + [hbm] * 4,
        out_specs=(vmem,) * 4,
        scratch_shapes=[
            pltpu.VMEM((32, TOK), BF),
            pltpu.VMEM((NY, 32, TOK), BF),
            pltpu.VMEM((2, NY, TOK, HD), BF),
            pltpu.VMEM((2, NY, TOK, HD), BF),
            pltpu.VMEM((4, NY, 4, 16, HD), BF),
            pltpu.VMEM((NP, NY, ROUNDS, 16, HD), BF),
            pltpu.VMEM((8, 2, NY, ROUNDS, 16, HD), BF),
            pltpu.VMEM((2, 32, HD), BF),
            pltpu.VMEM((NP, 2, 32, HD), BF),
            pltpu.VMEM((1024, HD), BF),
            pltpu.VMEM((1024, HD), BF),
            pltpu.VMEM((8, 2, NY, ROUNDS, 16, TOK), BF),
            pltpu.VMEM((4, NY, 4, ROUNDS, 16, TOK), BF),
            pltpu.VMEM((NP, NY, 16, TOK), BF),
            pltpu.VMEM((8, 2, NY, 16, TOK), BF),
            pltpu.VMEM((2, NY, HD, TOK), F32),
            pltpu.VMEM((2, HD, 512), F32),
            pltpu.VMEM((NP, 2, 32, HD), BF),
            pltpu.VMEM((NP, 2, 32, HD), BF),
            pltpu.VMEM((2, NY, TOK, HD), BF),
            pltpu.VMEM((2, NY, TOK, HD), BF),
        ]
        + [dma] * 9
        + [dma((4,))]
        + [dma] * 11,
        compiler_params=pltpu.CompilerParams(
            collective_id=0, has_side_effects=True, vmem_limit_bytes=48 * 1024 * 1024
        ),
        cost_estimate=pl.CostEstimate(flops=1_700_000_000, bytes_accessed=2_000_000, transcendentals=1_048_576),
    )(matches, active, global_pos, queries, key_rows, value_rows, cotangent)


def solution(mesh):
    rows = P(("batch", "seq"), None)
    return jax.shard_map(
        local,
        mesh=mesh,
        in_specs=(rows, rows, rows, rows, P("batch", None), P("batch", "seq"), P(("batch", "seq"))),
        out_specs=(rows,) * 4,
        check_vma=False,
    )
```

time: 1830 us -> 111 us (0.06)
  waiting for transfers between devices: 1400 us -> 0 us
  starting transfers between devices: 157 us -> 0 us
  local copies, waits for them, and re-layouts: 114 us -> 7.37 us
  Pallas kernels: 0 us -> 102 us
  matrix products: 67.8 us -> 0 us
  other arithmetic: 63.8 us -> 0 us
    psum x1 -> x0, waiting for transfers between devices: 938 us -> none  [local(): lax.psum(jnp.concatenate([key_glob.reshape(glob_count, feat_width), value...]
    all_gather x2 -> x0, waiting for transfers between devices: 306 us -> none  [the longest x1 212 us: local(): lax.all_gather(picked_values, 'seq', axis=0, tiled=True)]
    all_to_all x20 -> x0, waiting for transfers between devices: 156 us -> none  [the longest x6 57.3 us: route_pair(): lax.all_to_all(lead_moved, 'seq', split_axis=0, concat_axis=0, tiled=True)]
    all_to_all x20 -> x0, starting transfers between devices: 156 us -> none  [the longest x4 40.9 us: route_pair(): lax.all_to_all(leading.reshape(shard_count, tok_rows // shard_count, feat...]
    pallas_call x0 -> x1, Pallas kernels: none -> 102 us  [local(): pl.pallas_call(kernel, out_shape=(out,) * 4, in_specs=[smem] * 3 + [hbm]...]
    dot_general x52 -> x0, matrix products: 67.8 us -> none  [the longest x8 14.9 us: head_pass(): jnp.einsum('qk,ke->qe', probs_low, value_one, preferred_element_type=jnp....]
    unnamed x122 -> x17, local copies, waits for them, and re-layouts: 51.3 us -> 7.37 us
    slice x6 -> x0, other arithmetic: 19.3 us -> none  [the longest x3 10 us: local(): send_keys[:, match_no]]
  transfers between devices with their start and end apart: 23 -> 0, of which waited for: 20 -> 0; matrix products, arithmetic and copies ran while one was open for 8% -> 0% of each run, Pallas kernels for 0% -> 0%
where the time goes in v1:
time: 111 us; the launch traced here: 110 us
  Pallas kernels  102 us (92%)
  local copies, waits for them, and re-layouts  7.37 us (7%)
    pallas_call x1, Pallas kernels, local(): pl.pallas_call(kernel, out_shape=(out,) * 4, in_specs=[smem] * 3 + [hbm]...  102 us
    unnamed x17, local copies, waits for them, and re-layouts  7.37 us

profile of v1, /device:TPU:1, one launch (start us, length us, event | category | flops | bytes accessed | tf_op | source)
XLA Modules:
  0.0 110.4 jit_solution(14373238912911258506)
XLA Ops:
  0.6 0.0 copy-start.5
  0.6 0.0 copy-start.4
  0.7 0.8 copy.11.active
  1.4 0.0 copy-done.5
  1.4 0.0 copy-done.4
  1.4 0.0 copy-start
  1.4 0.9 copy-done
  2.4 0.0 copy-start.1
  2.4 0.9 copy-done.1
  3.3 0.0 copy-start.2
  3.3 0.9 copy-done.2
  4.3 0.0 copy-start.3
  4.3 0.9 copy-done.3
  5.2 102.3 %shard_map.102 = (bf16[128,1024]{1,0:T(8,128)(2,1)S(1)}, bf16[128,1024]{1,0:T(8,128)(2,1)S(1)}, bf16[128,1024]{1,0:T(8,128)(2,1)S(1)}, bf16[128,1024]{1,0:T(8,128)(2,1)S(1)}) custom-call(s32[3,128]{1,0:T(4,128)S(1)} %copy-done.4, s32[3,1]{1,0:T(4,128)S(1)} %copy.11.active, s32[4]{0:T(128)S(1)} %copy-done.5, bf16[128,1024]{1,0:T(8,128)(2,1)S(1)} %copy-done, ...), custom_call_target="tpu_custom_call" | custom-call | flops 1700000000 | bytes 2000000 | tf_op jit(solution)/shard_map/pallas_call | solution.py:272
  107.5 0.7 copy.16
  108.3 0.7 copy.17
  109.0 0.7 copy.18
  109.7 0.7 copy.19
Async XLA Ops:
  0.6 0.8 copy-start.5
  0.6 0.8 copy-start.4
  1.4 1.0 copy-start
  2.4 0.9 copy-start.1
  3.3 0.9 copy-start.2
  4.3 0.9 copy-start.3

commit v2 on v1

v2 whole, which is shorter than its diff:
```python
import jax
import jax.numpy as jnp
from jax import lax
from jax.experimental import pallas as pl
from jax.experimental.pallas import tpu as pltpu
from jax.sharding import PartitionSpec as P

HD = 128
ROUNDS = 3
NY = 8
NP = 16
TOK = 128
SCALE = HD**-0.5
LOG2E = 1.4426950408889634
BF = jnp.bfloat16
F32 = jnp.float32


def mm(a, b):
    return lax.dot_general(a, b, (((1,), (0,)), ((), ())), preferred_element_type=F32)


def mm_t(a, b):
    return lax.dot_general(a, b, (((1,), (1,)), ((), ())), preferred_element_type=F32)


def kernel(
    matches, active, gpos, q_in, k_in, v_in, g_in,
    o_out, dq_out, dk_out, dv_out,
    aux, aux_all, kv, qg, inter, stage, part, gl_mine, gl_all,
    k_loc, k_glob, v_loc, v_glob, probs, low, sgrad, q_t, g_t,
    ret_stage, ret, tot_stage, tot, own, gg_stage, gg, gsum, od_stage, kvg_stage,
    sem_aux, sem_kv, sem_qg, sem_inter, sem_part, sem_gl, sem_ret, sem_tot, sem_gg, sem_out,
    send_aux, send_kv, send_qg, send_inter, send_part, send_gl, send_ret, send_tot, send_gg, send_od, send_kvg,
):
    me = lax.axis_index("seq")
    my_x, my_y, my_zc = me // 32, (me // 4) % NY, me % 4
    my_z, my_core = my_zc // 2, my_zc % 2
    my_p = my_x * 4 + my_zc

    def shard(p, y):
        return (p // 4) * 32 + y * 4 + p % 4

    def line(y):
        return {"seq": shard(my_p, y)}

    def plane(p):
        return {"seq": shard(p, my_y)}

    def line_step(n):
        return (n + 1) // 2 * (1 - 2 * ((n + 1) % 2))

    def line_to(n):
        return (my_y + NY + line_step(n)) % NY

    def line_from(n):
        return (my_y + NY - line_step(n)) % NY

    def plane_to(n):
        return (my_x + n) % 4 * 4 + (my_zc + n + n // 4) % 4

    def chip_to(n):
        return (my_x + n) % 4 * 2 + (my_z + n + n // 4) % 2

    def put(src, dst, send, recv, where):
        pltpu.make_async_remote_copy(
            src_ref=src, dst_ref=dst, send_sem=send, recv_sem=recv, device_id=where,
            device_id_type=pl.DeviceIdType.MESH,
        ).start()

    def keep(src, dst, recv):
        pltpu.make_async_copy(src, dst, recv).start()

    def wait(ref, sem):
        pltpu.make_async_copy(ref, ref, sem).wait()

    def cols(ref, y):
        return ref.at[:, pl.ds(pl.multiple_of(y * HD, HD), HD)]

    def to_keepers(which, src, dst, send, recv):
        @pl.loop(0, 8)
        def _(i):
            tile = chip_to(i)
            here = jnp.logical_and(i == 0, my_core == which)

            @pl.when(here)
            def _():
                keep(src(tile), dst, recv)

            @pl.when(jnp.logical_not(here))
            def _():
                put(src(tile), dst, send, recv, plane(tile * 2 + which))

    barrier = pltpu.get_barrier_semaphore()

    @pl.loop(1, NY)
    def _(n):
        pl.semaphore_signal(barrier, inc=1, device_id=line(line_to(n)), device_id_type=pl.DeviceIdType.MESH)

    @pl.loop(1, NP)
    def _(n):
        pl.semaphore_signal(barrier, inc=1, device_id=plane(plane_to(n)), device_id_type=pl.DeviceIdType.MESH)

    row = lax.broadcasted_iota(jnp.int32, (32, TOK), 0)
    lane = lax.broadcasted_iota(jnp.int32, (32, TOK), 1)
    tile = jnp.zeros((32, TOK), F32)
    for n in range(4):
        here = (row == (my_y % 4) * 4 + n) & (lane == gpos[n] - me * TOK)
        tile = jnp.where(here, 1.0, tile)
    for r in range(ROUNDS):
        tile = jnp.where(row == 16 + r, active[r].astype(F32), tile)
    aux[...] = tile.astype(BF)

    pl.semaphore_wait(barrier, NY - 1 + NP - 1)

    @pl.loop(1, NY)
    def _(n):
        put(cols(k_in, line_to(n)), kv.at[0, my_y], send_kv, sem_kv.at[0, my_y], line(line_to(n)))

    keep(cols(k_in, my_y), kv.at[0, my_y], sem_kv.at[0, my_y])
    keep(cols(v_in, my_y), kv.at[1, my_y], sem_kv.at[1, my_y])
    keep(cols(q_in, my_y), qg.at[0, my_y], sem_qg.at[0])
    keep(cols(g_in, my_y), qg.at[1, my_y], sem_qg.at[1])
    keep(aux, aux_all.at[my_y], sem_aux)

    @pl.loop(1, NY)
    def _(n):
        put(aux, aux_all.at[my_y], send_aux, sem_aux, line(line_to(n)))

    def hand_on(which, t):
        wait(kv.at[which, t], sem_kv.at[which, t])
        to_keepers(
            which,
            lambda tile: kv.at[which, t, pl.ds(pl.multiple_of(tile * 16, 16), 16), :],
            inter.at[shard(my_p, t)], send_inter, sem_inter,
        )

    def pick_and_send():
        wait(inter, sem_inter)

        def pick(p):
            for t in range(NY):
                for r in range(ROUNDS):
                    stage[p, t, r] = inter[matches[r, shard(p, t)]]

        dst, sem = part.at[my_p // 2, my_core], sem_part.at[my_core]

        @pl.loop(1, NP)
        def _(n):
            p = plane_to(n)
            pick(p)
            put(stage.at[p], dst, send_part, sem, plane(p))

        pick(my_p)
        keep(stage.at[my_p], dst, sem)

    @pl.loop(0, NY)
    def _(n):
        hand_on(0, line_from(n))

        @pl.when(n > 0)
        def _():
            put(cols(v_in, line_to(n)), kv.at[1, my_y], send_kv, sem_kv.at[1, my_y], line(line_to(n)))

    @pl.when(my_core == 0)
    def _():
        pick_and_send()

    @pl.loop(0, NY)
    def _(n):
        hand_on(1, line_from(n))

        @pl.when(n > 0)
        def _():
            put(cols(q_in, line_to(n)), qg.at[0, my_y], send_qg, sem_qg.at[0], line(line_to(n)))

    @pl.loop(1, NY)
    def _(n):
        put(cols(g_in, line_to(n)), qg.at[1, my_y], send_qg, sem_qg.at[1], line(line_to(n)))

    wait(aux_all, sem_aux)
    for half in range(2):
        picks = jnp.concatenate([aux_all[half * 4 + n, :16] for n in range(4)], axis=1)
        for which in range(2):
            rows = kv[which, half * 4 : half * 4 + 4].reshape(4 * TOK, HD)
            gl_mine[which, half * 16 : half * 16 + 16] = mm(picks, rows).astype(BF)
    keep(gl_mine, gl_all.at[my_p], sem_gl)

    @pl.loop(1, NP)
    def _(n):
        put(gl_mine, gl_all.at[my_p], send_gl, sem_gl, plane(plane_to(n)))

    @pl.when(my_core == 1)
    def _():
        pick_and_send()

    wait(gl_all, sem_gl)
    k_glob[...] = gl_all[:, 0].reshape(512, HD)
    v_glob[...] = gl_all[:, 1].reshape(512, HD)
    wait(qg.at[0], sem_qg.at[0])
    wait(part.at[:, 0], sem_part.at[0])

    @pl.loop(0, NY)
    def _(t):
        q = qg[0, t]
        k_loc[t, 0:TOK] = kv[0, t]
        for r in range(ROUNDS):
            k_loc[t, TOK * (r + 1) : TOK * (r + 2)] = part[:, 0, t, r].reshape(TOK, HD)
        flags = aux_all[t, 16:32].astype(F32)
        bias = jnp.concatenate(
            [jnp.zeros((1, TOK), F32)] + [(flags[r : r + 1] - 1.0) * 1e30 for r in range(ROUNDS)], axis=1
        )
        s_loc = mm_t(q, k_loc[t]) * (SCALE * LOG2E) + bias
        s_glob = mm_t(q, k_glob[...]) * (SCALE * LOG2E)
        peak = jnp.maximum(jnp.max(s_loc, axis=1, keepdims=True), jnp.max(s_glob, axis=1, keepdims=True))
        w_loc, w_glob = jnp.exp2(s_loc - peak), jnp.exp2(s_glob - peak)
        inverse = 1.0 / (jnp.sum(w_loc, axis=1, keepdims=True) + jnp.sum(w_glob, axis=1, keepdims=True))
        p_loc, p_glob = w_loc * inverse, w_glob * inverse
        rows = pl.ds(pl.multiple_of(t * TOK, TOK), TOK)
        probs[rows, :512] = p_loc
        probs[rows, 512:] = p_glob
        low[rows, :512] = p_loc.astype(BF)
        low[rows, 512:] = p_glob.astype(BF)

    def give_back(which, t, term):
        own[which, t] = term[:, :TOK]
        for r in range(ROUNDS):
            ret_stage[:, which, t, r] = term[:, TOK * (r + 1) : TOK * (r + 2)].astype(BF).reshape(8, 16, TOK)
        to_keepers(
            which, lambda tile: ret_stage.at[tile, which, t], ret.at[shard(my_p, t)], send_ret, sem_ret
        )

    def give_globals(which, term):
        gg_stage[which] = term.T.astype(BF).reshape(NP, 32, HD)
        keep(gg_stage.at[which, my_p], gg.at[which, my_p], sem_gg.at[which])

        @pl.loop(1, NP)
        def _(n):
            p = plane_to(n)
            put(gg_stage.at[which, p], gg.at[which, my_p], send_gg, sem_gg.at[which], plane(p))

    wait(qg.at[1], sem_qg.at[1])

    @pl.loop(0, NY)
    def _(t):
        rows = pl.ds(pl.multiple_of(t * TOK, TOK), TOK)
        gt = qg[1, t].T
        g_t[:, rows] = gt
        give_back(1, t, mm(gt, low[rows, :512]))

    give_globals(1, mm(g_t[...], low[:, 512:]))

    wait(part.at[:, 1], sem_part.at[1])

    @pl.loop(0, NY)
    def _(n):
        t = line_to(n)
        rows = pl.ds(pl.multiple_of(t * TOK, TOK), TOK)
        q, g = qg[0, t], qg[1, t]
        v_loc[0:TOK] = kv[1, t]
        for r in range(ROUNDS):
            v_loc[TOK * (r + 1) : TOK * (r + 2)] = part[:, 1, t, r].reshape(TOK, HD)
        gp_loc, gp_glob = mm_t(g, v_loc[...]), mm_t(g, v_glob[...])
        low_loc, low_glob = low[rows, :512], low[rows, 512:]
        centre = jnp.sum(low_loc.astype(F32) * gp_loc, axis=1, keepdims=True) + jnp.sum(
            low_glob.astype(F32) * gp_glob, axis=1, keepdims=True
        )
        sg_loc = (probs[rows, :512] * (gp_loc - centre)).astype(BF)
        sg_glob = (probs[rows, 512:] * (gp_glob - centre)).astype(BF)
        sgrad[rows] = sg_glob
        qt = q.T
        q_t[:, rows] = qt
        give_back(0, t, mm(qt, sg_loc) * SCALE)
        od_stage[0, t] = (mm(low_loc, v_loc[...]) + mm(low_glob, v_glob[...])).astype(BF)
        od_stage[1, t] = ((mm(sg_loc, k_loc[t]) + mm(sg_glob, k_glob[...])) * SCALE).astype(BF)

        @pl.when(n == 0)
        def _():
            keep(od_stage.at[0, t], cols(o_out, my_y), sem_out.at[0])
            keep(od_stage.at[1, t], cols(dq_out, my_y), sem_out.at[1])

        @pl.when(n > 0)
        def _():
            put(od_stage.at[0, t], cols(o_out, my_y), send_od, sem_out.at[0], line(t))
            put(od_stage.at[1, t], cols(dq_out, my_y), send_od, sem_out.at[1], line(t))

    give_globals(0, mm(q_t[...], sgrad[...]) * SCALE)

    def add_and_send():
        wait(ret, sem_ret)

        @pl.loop(0, NY)
        def _(n):
            t = line_to(n)
            dst, sem = tot.at[my_p // 2, my_core, t], sem_tot.at[my_core, t]

            @pl.loop(0, NP)
            def _(i):
                p = plane_to(i)
                terms = [ret[matches[r, shard(p, t)], r].astype(F32) for r in range(ROUNDS)]
                tot_stage[p, t] = (terms[0] + terms[1] + terms[2]).astype(BF)

                @pl.when(i == 0)
                def _():
                    keep(tot_stage.at[p, t], dst, sem)

                @pl.when(i > 0)
                def _():
                    put(tot_stage.at[p, t], dst, send_tot, sem, plane(p))

    def finish(which, out):
        wait(gg.at[which], sem_gg.at[which])
        gsum[...] = jnp.sum(gg[which].astype(F32), axis=0).astype(BF)

        @pl.loop(0, NY)
        def _(n):
            t = line_to(n)
            wait(tot.at[:, which, t], sem_tot.at[which, t])
            rows = gsum[pl.ds(pl.multiple_of((t // 4) * 16, 16), 16)]
            back = own[which, t] + tot[:, which, t].reshape(HD, TOK).astype(F32)
            there = lax.dot_general(aux_all[t, :16], rows, (((0,), (0,)), ((), ())), preferred_element_type=F32)
            kvg_stage[which, t] = (back.T + there).astype(BF)

            @pl.when(n == 0)
            def _():
                keep(kvg_stage.at[which, t], cols(out, my_y), sem_out.at[2 + which])

            @pl.when(n > 0)
            def _():
                put(kvg_stage.at[which, t], cols(out, my_y), send_kvg, sem_out.at[2 + which], line(t))

    @pl.when(my_core == 1)
    def _():
        add_and_send()

    finish(1, dv_out)

    @pl.when(my_core == 0)
    def _():
        add_and_send()

    finish(0, dk_out)

    for n, out in enumerate((o_out, dq_out, dk_out, dv_out)):
        wait(out, sem_out.at[n])
    wait(aux_all.at[: NY - 1], send_aux)
    for sem in (send_kv, send_qg, send_od, send_kvg):
        wait(kv.at[:, : NY - 1], sem)
    for sem in (send_inter, send_tot):
        wait(tot_stage.at[: NP - 1], sem)
    for sem in (send_part, send_ret):
        wait(stage.at[: NP - 1], sem)
    wait(gl_all.at[: NP - 1], send_gl)
    wait(gl_all.at[: NP - 1], send_gg)


def hand_out(*refs):
    ins, outs, held, sems = refs[:4], refs[4:8], refs[8], refs[9]
    come = [pltpu.make_async_copy(a, held.at[n], sems.at[0, n]) for n, a in enumerate(ins)]
    go = [pltpu.make_async_copy(held.at[n], b, sems.at[1, n]) for n, b in enumerate(outs)]
    for copy in come:
        copy.start()
    for n in range(4):
        come[n].wait()
        go[n].start()
    for copy in go:
        copy.wait()


def local(queries, key_rows, value_rows, cotangent, matches, active, global_pos):
    out = jax.ShapeDtypeStruct(queries.shape, BF)
    smem, hbm = (pl.BlockSpec(memory_space=m) for m in (pltpu.SMEM, pltpu.HBM))
    dma = pltpu.SemaphoreType.DMA
    shapes = [
        ((32, TOK), BF),
        ((NY, 32, TOK), BF),
        ((2, NY, TOK, HD), BF),
        ((2, NY, TOK, HD), BF),
        ((NP * NY, 16, HD), BF),
        ((NP, NY, ROUNDS, 16, HD), BF),
        ((8, 2, NY, ROUNDS, 16, HD), BF),
        ((2, 32, HD), BF),
        ((NP, 2, 32, HD), BF),
        ((NY, 512, HD), BF),
        ((512, HD), BF),
        ((512, HD), BF),
        ((512, HD), BF),
        ((NY * TOK, 1024), F32),
        ((NY * TOK, 1024), BF),
        ((NY * TOK, 512), BF),
        ((HD, NY * TOK), BF),
        ((HD, NY * TOK), BF),
        ((8, 2, NY, ROUNDS, 16, TOK), BF),
        ((NP * NY, ROUNDS, 16, TOK), BF),
        ((NP, NY, 16, TOK), BF),
        ((8, 2, NY, 16, TOK), BF),
        ((2, NY, HD, TOK), F32),
        ((2, NP, 32, HD), BF),
        ((2, NP, 32, HD), BF),
        ((32, HD), BF),
        ((2, NY, TOK, HD), BF),
        ((2, NY, TOK, HD), BF),
    ]
    results = pl.pallas_call(
        kernel,
        out_shape=(out,) * 4,
        in_specs=[smem] * 3 + [hbm] * 4,
        out_specs=(hbm,) * 4,
        scratch_shapes=[pltpu.VMEM(*s) for s in shapes]
        + [dma, dma((2, NY)), dma((2,)), dma, dma((2,)), dma, dma, dma((2, NY)), dma((2,)), dma((4,))]
        + [dma] * 11,
        compiler_params=pltpu.CompilerParams(
            collective_id=0, has_side_effects=True, vmem_limit_bytes=63 * 1024 * 1024
        ),
        cost_estimate=pl.CostEstimate(flops=1_700_000_000, bytes_accessed=2_000_000, transcendentals=1_048_576),
    )(matches, active.reshape(ROUNDS), global_pos, queries, key_rows, value_rows, cotangent)
    return pl.pallas_call(
        hand_out,
        out_shape=(out,) * 4,
        in_specs=[hbm] * 4,
        out_specs=(hbm,) * 4,
        scratch_shapes=[pltpu.VMEM((4, TOK, NY * HD), BF), dma((2, 4))],
        compiler_params=pltpu.CompilerParams(vmem_limit_bytes=63 * 1024 * 1024),
    )(*results)


def solution(mesh):
    rows = P(("batch", "seq"), None)
    return jax.shard_map(
        local,
        mesh=mesh,
        in_specs=(rows, rows, rows, rows, P("batch", None), P("batch", "seq"), P(("batch", "seq"))),
        out_specs=(rows,) * 4,
        check_vma=False,
    )
```

time: 111 us -> 93.7 us (0.84)
  Pallas kernels: 102 us -> 92.8 us
  local copies, waits for them, and re-layouts: 7.37 us -> 0 us
    pallas_call x1, Pallas kernels: 102 us -> 90.8 us  [local(): pl.pallas_call(kernel, out_shape=(out,) * 4, in_specs=[smem] * 3 + [hbm]...]
    unnamed x17 -> x0, local copies, waits for them, and re-layouts: 7.37 us -> none
    pallas_call x0 -> x1, Pallas kernels: none -> 1.98 us  [local(): pl.pallas_call(hand_out, out_shape=(out,) * 4, in_specs=[hbm] * 4, out_sp...]
where the time goes in v2:
time: 93.7 us; the launch traced here: 93.5 us
  Pallas kernels  92.8 us (99%)
    pallas_call x1, Pallas kernels, local(): pl.pallas_call(kernel, out_shape=(out,) * 4, in_specs=[smem] * 3 + [hbm]...  90.8 us
    pallas_call x1, Pallas kernels, local(): pl.pallas_call(hand_out, out_shape=(out,) * 4, in_specs=[hbm] * 4, out_sp...  1.98 us

profile of v2, /device:TPU:1, one launch (start us, length us, event | category | flops | bytes accessed | tf_op | source)
XLA Modules:
  0.0 93.5 jit_solution(8706769641244655656)
XLA Ops:
  0.6 90.8 %shard_map.102 = (bf16[128,1024]{1,0:T(8,128)(2,1)}, bf16[128,1024]{1,0:T(8,128)(2,1)}, bf16[128,1024]{1,0:T(8,128)(2,1)}, bf16[128,1024]{1,0:T(8,128)(2,1)}) custom-call(s32[3,128]{1,0:T(4,128)} %matches.1, s32[3]{0:T(128)} %bitcast.1, s32[4]{0:T(128)} %gpos.1, bf16[128,1024]{1,0:T(8,128)(2,1)} %q_in.1, bf16[128,1024]{1,0:T(8,128)(2,1)} %k_in.1, ...), custom_call_target="tpu_custom_call" | custom-call | flops 1700000000 | bytes 2000000 | tf_op jit(solution)/shard_map/pallas_call | solution.py:404
  91.5 2.0 %shard_map.103 = (bf16[128,1024]{1,0:T(8,128)(2,1)}, bf16[128,1024]{1,0:T(8,128)(2,1)}, bf16[128,1024]{1,0:T(8,128)(2,1)}, bf16[128,1024]{1,0:T(8,128)(2,1)}) custom-call(bf16[128,1024]{1,0:T(8,128)(2,1)} %get-tuple-element.8.refs_0_, bf16[128,1024]{1,0:T(8,128)(2,1)} %get-tuple-element.9.refs_1_, bf16[128,1024]{1,0:T(8,128)(2,1)} %get-tuple-element.10.refs_2_, ...), custom_call_target="tpu_custom_call" | custom-call | tf_op jit(solution)/shard_map/pallas_call | solution.py:417

commit v3 on v2

--- a/solution.py
+++ b/solution.py
@@ -9,6 +9,7 @@
 ROUNDS = 3
 NY = 8
 NP = 16
+EARLY = 4
 TOK = 128
 SCALE = HD**-0.5
 LOG2E = 1.4426950408889634
@@ -27,16 +28,17 @@
 def kernel(
     matches, active, gpos, q_in, k_in, v_in, g_in,
     o_out, dq_out, dk_out, dv_out,
-    aux, aux_all, kv, qg, inter, stage, part, gl_mine, gl_all,
+    moved, aux, aux_all, kv, qg, inter, stage, part, gl_mine, gl_all,
     k_loc, k_glob, v_loc, v_glob, probs, low, sgrad, q_t, g_t,
-    ret_stage, ret, tot_stage, tot, own, gg_stage, gg, gsum, od_stage, kvg_stage,
-    sem_aux, sem_kv, sem_qg, sem_inter, sem_part, sem_gl, sem_ret, sem_tot, sem_gg, sem_out,
+    ret_stage, ret, tot_stage, tot, own, gg_stage, gg_half, gg_pair, gg_sum, gg, gsum, od_stage, kvg_stage,
+    sem_moved, sem_aux, sem_kv, sem_qg, sem_inter, sem_part, sem_gl, sem_ret, sem_tot, sem_gg, sem_out,
     send_aux, send_kv, send_qg, send_inter, send_part, send_gl, send_ret, send_tot, send_gg, send_od, send_kvg,
 ):
     me = lax.axis_index("seq")
     my_x, my_y, my_zc = me // 32, (me // 4) % NY, me % 4
     my_z, my_core = my_zc // 2, my_zc % 2
     my_p = my_x * 4 + my_zc
+    my_chip = my_p // 2
 
     def shard(p, y):
         return (p // 4) * 32 + y * 4 + p % 4
@@ -58,6 +60,12 @@
 
     def plane_to(n):
         return (my_x + n) % 4 * 4 + (my_zc + n + n // 4) % 4
+
+    def turn(n):
+        return line_to((n + 1) % NY)
+
+    def far(n):
+        return line_to(NY - 1 - n)
 
     def chip_to(n):
         return (my_x + n) % 4 * 2 + (my_z + n + n // 4) % 2
@@ -100,6 +108,12 @@
     @pl.loop(1, NP)
     def _(n):
         pl.semaphore_signal(barrier, inc=1, device_id=plane(plane_to(n)), device_id_type=pl.DeviceIdType.MESH)
+
+    for n, ref in enumerate((k_in, v_in, q_in, g_in)):
+
+        @pl.loop(0, NY)
+        def _(y):
+            keep(cols(ref, y), moved.at[n, y], sem_moved.at[n])
 
     row = lax.broadcasted_iota(jnp.int32, (32, TOK), 0)
     lane = lax.broadcasted_iota(jnp.int32, (32, TOK), 1)
@@ -110,17 +124,19 @@
     for r in range(ROUNDS):
         tile = jnp.where(row == 16 + r, active[r].astype(F32), tile)
     aux[...] = tile.astype(BF)
+    for n in range(4):
+        wait(moved.at[n], sem_moved.at[n])
 
     pl.semaphore_wait(barrier, NY - 1 + NP - 1)
 
     @pl.loop(1, NY)
     def _(n):
-        put(cols(k_in, line_to(n)), kv.at[0, my_y], send_kv, sem_kv.at[0, my_y], line(line_to(n)))
-
-    keep(cols(k_in, my_y), kv.at[0, my_y], sem_kv.at[0, my_y])
-    keep(cols(v_in, my_y), kv.at[1, my_y], sem_kv.at[1, my_y])
-    keep(cols(q_in, my_y), qg.at[0, my_y], sem_qg.at[0])
-    keep(cols(g_in, my_y), qg.at[1, my_y], sem_qg.at[1])
+        put(moved.at[0, line_to(n)], kv.at[0, my_y], send_kv, sem_kv.at[0, my_y], line(line_to(n)))
+
+    keep(moved.at[0, my_y], kv.at[0, my_y], sem_kv.at[0, my_y])
+    keep(moved.at[1, my_y], kv.at[1, my_y], sem_kv.at[1, my_y])
+    keep(moved.at[2, my_y], qg.at[0, my_y], sem_qg.at[0])
+    keep(moved.at[3, my_y], qg.at[1, my_y], sem_qg.at[1])
     keep(aux, aux_all.at[my_y], sem_aux)
 
     @pl.loop(1, NY)
@@ -138,21 +154,21 @@
     def pick_and_send():
         wait(inter, sem_inter)
 
-        def pick(p):
-            for t in range(NY):
+        @pl.loop(0, NY)
+        def _(n):
+            named = [[matches[r, shard(p, turn(n))] for r in range(ROUNDS)] for p in range(NP)]
+            for p in range(NP):
                 for r in range(ROUNDS):
-                    stage[p, t, r] = inter[matches[r, shard(p, t)]]
-
-        dst, sem = part.at[my_p // 2, my_core], sem_part.at[my_core]
-
-        @pl.loop(1, NP)
-        def _(n):
-            p = plane_to(n)
-            pick(p)
-            put(stage.at[p], dst, send_part, sem, plane(p))
-
-        pick(my_p)
-        keep(stage.at[my_p], dst, sem)
+                    stage[p, n, r] = inter[named[p][r]]
+
+            dst, sem = part.at[my_chip, my_core, n], sem_part.at[my_core, n]
+
+            @pl.loop(1, NP)
+            def _(i):
+                p = plane_to(i)
+                put(stage.at[p, n], dst, send_part, sem, plane(p))
+
+            keep(stage.at[my_p, n], dst, sem)
 
     @pl.loop(0, NY)
     def _(n):
@@ -160,7 +176,7 @@
 
         @pl.when(n > 0)
         def _():
-            put(cols(v_in, line_to(n)), kv.at[1, my_y], send_kv, sem_kv.at[1, my_y], line(line_to(n)))
+            put(moved.at[1, line_to(n)], kv.at[1, my_y], send_kv, sem_kv.at[1, my_y], line(line_to(n)))
 
     @pl.when(my_core == 0)
     def _():
@@ -172,11 +188,11 @@
 
         @pl.when(n > 0)
         def _():
-            put(cols(q_in, line_to(n)), qg.at[0, my_y], send_qg, sem_qg.at[0], line(line_to(n)))
+            put(moved.at[2, line_to(n)], qg.at[0, my_y], send_qg, sem_qg.at[0], line(line_to(n)))
 
     @pl.loop(1, NY)
     def _(n):
-        put(cols(g_in, line_to(n)), qg.at[1, my_y], send_qg, sem_qg.at[1], line(line_to(n)))
+        put(moved.at[3, line_to(n)], qg.at[1, my_y], send_qg, sem_qg.at[1], line(line_to(n)))
 
     wait(aux_all, sem_aux)
     for half in range(2):
@@ -184,28 +200,31 @@
         for which in range(2):
             rows = kv[which, half * 4 : half * 4 + 4].reshape(4 * TOK, HD)
             gl_mine[which, half * 16 : half * 16 + 16] = mm(picks, rows).astype(BF)
-    keep(gl_mine, gl_all.at[my_p], sem_gl)
-
-    @pl.loop(1, NP)
-    def _(n):
-        put(gl_mine, gl_all.at[my_p], send_gl, sem_gl, plane(plane_to(n)))
+    keep(gl_mine, gl_all.at[my_core, my_chip], sem_gl.at[0])
+
+    @pl.loop(1, 8)
+    def _(n):
+        put(gl_mine, gl_all.at[my_core, my_chip], send_gl.at[0], sem_gl.at[0], plane(chip_to(n) * 2 + my_core))
 
     @pl.when(my_core == 1)
     def _():
         pick_and_send()
 
-    wait(gl_all, sem_gl)
-    k_glob[...] = gl_all[:, 0].reshape(512, HD)
-    v_glob[...] = gl_all[:, 1].reshape(512, HD)
+    wait(gl_all.at[0], sem_gl.at[0])
+    put(gl_all.at[my_core], gl_all.at[my_core], send_gl.at[1], sem_gl.at[1], plane(my_p + 1 - 2 * my_core))
+    wait(gl_all.at[0], sem_gl.at[1])
+    k_glob[...] = gl_all[:, :, 0].reshape(512, HD)
+    v_glob[...] = gl_all[:, :, 1].reshape(512, HD)
     wait(qg.at[0], sem_qg.at[0])
-    wait(part.at[:, 0], sem_part.at[0])
 
     @pl.loop(0, NY)
-    def _(t):
+    def _(n):
+        t = turn(n)
+        wait(part.at[:, 0, n], sem_part.at[0, n])
         q = qg[0, t]
         k_loc[t, 0:TOK] = kv[0, t]
         for r in range(ROUNDS):
-            k_loc[t, TOK * (r + 1) : TOK * (r + 2)] = part[:, 0, t, r].reshape(TOK, HD)
+            k_loc[t, TOK * (r + 1) : TOK * (r + 2)] = part[:, 0, n, r].reshape(TOK, HD)
         flags = aux_all[t, 16:32].astype(F32)
         bias = jnp.concatenate(
             [jnp.zeros((1, TOK), F32)] + [(flags[r : r + 1] - 1.0) * 1e30 for r in range(ROUNDS)], axis=1
@@ -222,22 +241,33 @@
         low[rows, :512] = p_loc.astype(BF)
         low[rows, 512:] = p_glob.astype(BF)
 
-    def give_back(which, t, term):
+    def send_back(which, t):
+        to_keepers(which, lambda tile: ret_stage.at[tile, which, t], ret.at[shard(my_p, t)], send_ret, sem_ret)
+
+    def set_terms(which, t, term):
         own[which, t] = term[:, :TOK]
         for r in range(ROUNDS):
             ret_stage[:, which, t, r] = term[:, TOK * (r + 1) : TOK * (r + 2)].astype(BF).reshape(8, 16, TOK)
-        to_keepers(
-            which, lambda tile: ret_stage.at[tile, which, t], ret.at[shard(my_p, t)], send_ret, sem_ret
+
+    def share_globals(which, term):
+        gg_stage[which] = term.T.reshape(2, 8, 32, HD)
+        gg_half[which] = gg_stage[which, 1 - my_core].astype(BF)
+        put(
+            gg_half.at[which], gg_pair.at[which], send_gg.at[0], sem_gg.at[0, which], plane(my_p + 1 - 2 * my_core)
         )
 
-    def give_globals(which, term):
-        gg_stage[which] = term.T.astype(BF).reshape(NP, 32, HD)
-        keep(gg_stage.at[which, my_p], gg.at[which, my_p], sem_gg.at[which])
-
-        @pl.loop(1, NP)
+    def give_globals(which):
+        wait(gg_pair.at[which], sem_gg.at[0, which])
+        gg_sum[which] = (gg_stage[which, my_core] + gg_pair[which].astype(F32)).astype(BF)
+        keep(gg_sum.at[which, my_chip], gg.at[which, my_chip], sem_gg.at[1, which])
+
+        @pl.loop(1, 8)
         def _(n):
-            p = plane_to(n)
-            put(gg_stage.at[which, p], gg.at[which, my_p], send_gg, sem_gg.at[which], plane(p))
+            chip = chip_to(n)
+            put(
+                gg_sum.at[which, chip], gg.at[which, my_chip], send_gg.at[1], sem_gg.at[1, which],
+                plane(chip * 2 + my_core),
+            )
 
     wait(qg.at[1], sem_qg.at[1])
 
@@ -246,20 +276,20 @@
         rows = pl.ds(pl.multiple_of(t * TOK, TOK), TOK)
         gt = qg[1, t].T
         g_t[:, rows] = gt
-        give_back(1, t, mm(gt, low[rows, :512]))
-
-    give_globals(1, mm(g_t[...], low[:, 512:]))
-
-    wait(part.at[:, 1], sem_part.at[1])
+        set_terms(1, t, mm(gt, low[rows, :512]))
+        send_back(1, t)
+
+    share_globals(1, mm(g_t[...], low[:, 512:]))
 
     @pl.loop(0, NY)
     def _(n):
-        t = line_to(n)
+        t = turn(n)
+        wait(part.at[:, 1, n], sem_part.at[1, n])
         rows = pl.ds(pl.multiple_of(t * TOK, TOK), TOK)
         q, g = qg[0, t], qg[1, t]
         v_loc[0:TOK] = kv[1, t]
         for r in range(ROUNDS):
-            v_loc[TOK * (r + 1) : TOK * (r + 2)] = part[:, 1, t, r].reshape(TOK, HD)
+            v_loc[TOK * (r + 1) : TOK * (r + 2)] = part[:, 1, n, r].reshape(TOK, HD)
         gp_loc, gp_glob = mm_t(g, v_loc[...]), mm_t(g, v_glob[...])
         low_loc, low_glob = low[rows, :512], low[rows, 512:]
         centre = jnp.sum(low_loc.astype(F32) * gp_loc, axis=1, keepdims=True) + jnp.sum(
@@ -270,69 +300,78 @@
         sgrad[rows] = sg_glob
         qt = q.T
         q_t[:, rows] = qt
-        give_back(0, t, mm(qt, sg_loc) * SCALE)
+        set_terms(0, t, mm(qt, sg_loc) * SCALE)
+
+        @pl.when(n < EARLY)
+        def _():
+            send_back(0, t)
+
         od_stage[0, t] = (mm(low_loc, v_loc[...]) + mm(low_glob, v_glob[...])).astype(BF)
         od_stage[1, t] = ((mm(sg_loc, k_loc[t]) + mm(sg_glob, k_glob[...])) * SCALE).astype(BF)
 
-        @pl.when(n == 0)
+        @pl.when(n == NY - 1)
         def _():
             keep(od_stage.at[0, t], cols(o_out, my_y), sem_out.at[0])
             keep(od_stage.at[1, t], cols(dq_out, my_y), sem_out.at[1])
 
-        @pl.when(n > 0)
+        @pl.when(n < NY - 1)
         def _():
             put(od_stage.at[0, t], cols(o_out, my_y), send_od, sem_out.at[0], line(t))
             put(od_stage.at[1, t], cols(dq_out, my_y), send_od, sem_out.at[1], line(t))
 
-    give_globals(0, mm(q_t[...], sgrad[...]) * SCALE)
-
     def add_and_send():
         wait(ret, sem_ret)
 
         @pl.loop(0, NY)
         def _(n):
-            t = line_to(n)
+            t = far(n)
             dst, sem = tot.at[my_p // 2, my_core, t], sem_tot.at[my_core, t]
 
-            @pl.loop(0, NP)
+            named = [[matches[r, shard(p, t)] for r in range(ROUNDS)] for p in range(NP)]
+            for p in range(NP):
+                terms = [ret[named[p][r], r].astype(F32) for r in range(ROUNDS)]
+                tot_stage[p, t] = (terms[0] + terms[1] + terms[2]).astype(BF)
+
+            @pl.loop(1, NP)
             def _(i):
                 p = plane_to(i)
-                terms = [ret[matches[r, shard(p, t)], r].astype(F32) for r in range(ROUNDS)]
-                tot_stage[p, t] = (terms[0] + terms[1] + terms[2]).astype(BF)
-
-                @pl.when(i == 0)
-                def _():
-                    keep(tot_stage.at[p, t], dst, sem)
-
-                @pl.when(i > 0)
-                def _():
-                    put(tot_stage.at[p, t], dst, send_tot, sem, plane(p))
+                put(tot_stage.at[p, t], dst, send_tot, sem, plane(p))
+
+            keep(tot_stage.at[my_p, t], dst, sem)
 
     def finish(which, out):
-        wait(gg.at[which], sem_gg.at[which])
+        wait(gg.at[which], sem_gg.at[1, which])
         gsum[...] = jnp.sum(gg[which].astype(F32), axis=0).astype(BF)
 
         @pl.loop(0, NY)
         def _(n):
-            t = line_to(n)
+            t = far(n)
             wait(tot.at[:, which, t], sem_tot.at[which, t])
             rows = gsum[pl.ds(pl.multiple_of((t // 4) * 16, 16), 16)]
             back = own[which, t] + tot[:, which, t].reshape(HD, TOK).astype(F32)
             there = lax.dot_general(aux_all[t, :16], rows, (((0,), (0,)), ((), ())), preferred_element_type=F32)
             kvg_stage[which, t] = (back.T + there).astype(BF)
 
-            @pl.when(n == 0)
+            @pl.when(n == NY - 1)
             def _():
                 keep(kvg_stage.at[which, t], cols(out, my_y), sem_out.at[2 + which])
 
-            @pl.when(n > 0)
+            @pl.when(n < NY - 1)
             def _():
                 put(kvg_stage.at[which, t], cols(out, my_y), send_kvg, sem_out.at[2 + which], line(t))
+
+    give_globals(1)
 
     @pl.when(my_core == 1)
     def _():
         add_and_send()
 
+    @pl.loop(EARLY, NY)
+    def _(n):
+        send_back(0, turn(n))
+
+    share_globals(0, mm(q_t[...], sgrad[...]) * SCALE)
+    give_globals(0)
     finish(1, dv_out)
 
     @pl.when(my_core == 0)
@@ -350,8 +389,10 @@
         wait(tot_stage.at[: NP - 1], sem)
     for sem in (send_part, send_ret):
         wait(stage.at[: NP - 1], sem)
-    wait(gl_all.at[: NP - 1], send_gl)
-    wait(gl_all.at[: NP - 1], send_gg)
+    wait(gl_all.at[0, :7], send_gl.at[0])
+    wait(gl_all.at[0], send_gl.at[1])
+    wait(gg_half, send_gg.at[0])
+    wait(gg.at[:, :7], send_gg.at[1])
 
 
 def hand_out(*refs):
@@ -372,6 +413,7 @@
     smem, hbm = (pl.BlockSpec(memory_space=m) for m in (pltpu.SMEM, pltpu.HBM))
     dma = pltpu.SemaphoreType.DMA
     shapes = [
+        ((4, NY, TOK, HD), BF),
         ((32, TOK), BF),
         ((NY, 32, TOK), BF),
         ((2, NY, TOK, HD), BF),
@@ -380,7 +422,7 @@
         ((NP, NY, ROUNDS, 16, HD), BF),
         ((8, 2, NY, ROUNDS, 16, HD), BF),
         ((2, 32, HD), BF),
-        ((NP, 2, 32, HD), BF),
+        ((2, 8, 2, 32, HD), BF),
         ((NY, 512, HD), BF),
         ((512, HD), BF),
         ((512, HD), BF),
@@ -395,8 +437,11 @@
         ((NP, NY, 16, TOK), BF),
         ((8, 2, NY, 16, TOK), BF),
         ((2, NY, HD, TOK), F32),
-        ((2, NP, 32, HD), BF),
-        ((2, NP, 32, HD), BF),
+        ((2, 2, 8, 32, HD), F32),
+        ((2, 8, 32, HD), BF),
+        ((2, 8, 32, HD), BF),
+        ((2, 8, 32, HD), BF),
+        ((2, 8, 32, HD), BF),
         ((32, HD), BF),
         ((2, NY, TOK, HD), BF),
         ((2, NY, TOK, HD), BF),
@@ -407,8 +452,9 @@
         in_specs=[smem] * 3 + [hbm] * 4,
         out_specs=(hbm,) * 4,
         scratch_shapes=[pltpu.VMEM(*s) for s in shapes]
-        + [dma, dma((2, NY)), dma((2,)), dma, dma((2,)), dma, dma, dma((2, NY)), dma((2,)), dma((4,))]
-        + [dma] * 11,
+        + [dma((4,)), dma, dma((2, NY)), dma((2,)), dma, dma((2, NY)), dma((2,)), dma, dma((2, NY)), dma((2, 2)), dma((4,))]
+        + [dma] * 5
+        + [dma((2,)), dma, dma, dma((2,)), dma, dma],
         compiler_params=pltpu.CompilerParams(
             collective_id=0, has_side_effects=True, vmem_limit_bytes=63 * 1024 * 1024
         ),

time: 93.7 us -> 87.3 us (0.932)
  Pallas kernels: 92.8 us -> 86.4 us
    pallas_call x1, Pallas kernels: 90.8 us -> 84.4 us  [local(): pl.pallas_call(kernel, out_shape=(out,) * 4, in_specs=[smem] * 3 + [hbm]...]
where the time goes in v3:
time: 87.3 us; the launch traced here: 87.1 us
  Pallas kernels  86.4 us (99%)
    pallas_call x1, Pallas kernels, local(): pl.pallas_call(kernel, out_shape=(out,) * 4, in_specs=[smem] * 3 + [hbm]...  84.4 us
    pallas_call x1, Pallas kernels, local(): pl.pallas_call(hand_out, out_shape=(out,) * 4, in_specs=[hbm] * 4, out_sp...  1.98 us

profile of v3, /device:TPU:1, one launch (start us, length us, event | category | flops | bytes accessed | tf_op | source)
XLA Modules:
  0.0 87.1 jit_solution(3031347352074408694)
XLA Ops:
  0.6 84.4 %shard_map.102 = (bf16[128,1024]{1,0:T(8,128)(2,1)}, bf16[128,1024]{1,0:T(8,128)(2,1)}, bf16[128,1024]{1,0:T(8,128)(2,1)}, bf16[128,1024]{1,0:T(8,128)(2,1)}) custom-call(s32[3,128]{1,0:T(4,128)} %matches.1, s32[3]{0:T(128)} %bitcast.1, s32[4]{0:T(128)} %gpos.1, bf16[128,1024]{1,0:T(8,128)(2,1)} %q_in.1, bf16[128,1024]{1,0:T(8,128)(2,1)} %k_in.1, ...), custom_call_target="tpu_custom_call" | custom-call | flops 1700000000 | bytes 2000000 | tf_op jit(solution)/shard_map/pallas_call | solution.py:449
  85.1 2.0 %shard_map.103 = (bf16[128,1024]{1,0:T(8,128)(2,1)}, bf16[128,1024]{1,0:T(8,128)(2,1)}, bf16[128,1024]{1,0:T(8,128)(2,1)}, bf16[128,1024]{1,0:T(8,128)(2,1)}) custom-call(bf16[128,1024]{1,0:T(8,128)(2,1)} %get-tuple-element.8.refs_0_, bf16[128,1024]{1,0:T(8,128)(2,1)} %get-tuple-element.9.refs_1_, bf16[128,1024]{1,0:T(8,128)(2,1)} %get-tuple-element.10.refs_2_, ...), custom_call_target="tpu_custom_call" | custom-call | tf_op jit(solution)/shard_map/pallas_call | solution.py:463

commit v4 on v3

--- a/solution.py
+++ b/solution.py
@@ -58,17 +58,36 @@
     def line_from(n):
         return (my_y + NY - line_step(n)) % NY
 
-    def plane_to(n):
-        return (my_x + n) % 4 * 4 + (my_zc + n + n // 4) % 4
+    def at(x_off, zc_off):
+        return (my_x + x_off) % 4 * 4 + (my_zc + zc_off) % 4
+
+    def each_other(do):
+        @pl.loop(0, 4)
+        def _(i):
+            do(at(2, i))
+
+        @pl.loop(0, 4)
+        def _(i):
+            do(at(1, i))
+            do(at(3, i))
+
+        @pl.loop(1, 4)
+        def _(i):
+            do(at(0, i))
+
+    def each_chip(do):
+        @pl.loop(0, 2)
+        def _(i):
+            for x_off in (2, 1, 3):
+                do((my_x + x_off) % 4 * 2 + (my_z + 1 + i) % 2)
+
+        do(my_x * 2 + 1 - my_z)
 
     def turn(n):
         return line_to((n + 1) % NY)
 
     def far(n):
         return line_to(NY - 1 - n)
-
-    def chip_to(n):
-        return (my_x + n) % 4 * 2 + (my_z + n + n // 4) % 2
 
     def put(src, dst, send, recv, where):
         pltpu.make_async_remote_copy(
@@ -86,18 +105,15 @@
         return ref.at[:, pl.ds(pl.multiple_of(y * HD, HD), HD)]
 
     def to_keepers(which, src, dst, send, recv):
-        @pl.loop(0, 8)
-        def _(i):
-            tile = chip_to(i)
-            here = jnp.logical_and(i == 0, my_core == which)
-
-            @pl.when(here)
-            def _():
-                keep(src(tile), dst, recv)
-
-            @pl.when(jnp.logical_not(here))
-            def _():
-                put(src(tile), dst, send, recv, plane(tile * 2 + which))
+        each_chip(lambda tile: put(src(tile), dst, send, recv, plane(tile * 2 + which)))
+
+        @pl.when(my_core == which)
+        def _():
+            keep(src(my_chip), dst, recv)
+
+        @pl.when(my_core != which)
+        def _():
+            put(src(my_chip), dst, send, recv, plane(my_chip * 2 + which))
 
     barrier = pltpu.get_barrier_semaphore()
 
@@ -105,9 +121,9 @@
     def _(n):
         pl.semaphore_signal(barrier, inc=1, device_id=line(line_to(n)), device_id_type=pl.DeviceIdType.MESH)
 
-    @pl.loop(1, NP)
-    def _(n):
-        pl.semaphore_signal(barrier, inc=1, device_id=plane(plane_to(n)), device_id_type=pl.DeviceIdType.MESH)
+    each_other(
+        lambda p: pl.semaphore_signal(barrier, inc=1, device_id=plane(p), device_id_type=pl.DeviceIdType.MESH)
+    )
 
     for n, ref in enumerate((k_in, v_in, q_in, g_in)):
 
@@ -163,11 +179,7 @@
 
             dst, sem = part.at[my_chip, my_core, n], sem_part.at[my_core, n]
 
-            @pl.loop(1, NP)
-            def _(i):
-                p = plane_to(i)
-                put(stage.at[p, n], dst, send_part, sem, plane(p))
-
+            each_other(lambda p: put(stage.at[p, n], dst, send_part, sem, plane(p)))
             keep(stage.at[my_p, n], dst, sem)
 
     @pl.loop(0, NY)
@@ -177,18 +189,23 @@
         @pl.when(n > 0)
         def _():
             put(moved.at[1, line_to(n)], kv.at[1, my_y], send_kv, sem_kv.at[1, my_y], line(line_to(n)))
+
+    @pl.loop(0, 4)
+    def _(n):
+        hand_on(1, line_from(n))
+
+        @pl.when(n > 0)
+        def _():
+            put(moved.at[2, line_to(n)], qg.at[0, my_y], send_qg, sem_qg.at[0], line(line_to(n)))
 
     @pl.when(my_core == 0)
     def _():
         pick_and_send()
 
-    @pl.loop(0, NY)
+    @pl.loop(4, NY)
     def _(n):
         hand_on(1, line_from(n))
-
-        @pl.when(n > 0)
-        def _():
-            put(moved.at[2, line_to(n)], qg.at[0, my_y], send_qg, sem_qg.at[0], line(line_to(n)))
+        put(moved.at[2, line_to(n)], qg.at[0, my_y], send_qg, sem_qg.at[0], line(line_to(n)))
 
     @pl.loop(1, NY)
     def _(n):
@@ -202,9 +219,11 @@
             gl_mine[which, half * 16 : half * 16 + 16] = mm(picks, rows).astype(BF)
     keep(gl_mine, gl_all.at[my_core, my_chip], sem_gl.at[0])
 
-    @pl.loop(1, 8)
-    def _(n):
-        put(gl_mine, gl_all.at[my_core, my_chip], send_gl.at[0], sem_gl.at[0], plane(chip_to(n) * 2 + my_core))
+    each_chip(
+        lambda chip: put(
+            gl_mine, gl_all.at[my_core, my_chip], send_gl.at[0], sem_gl.at[0], plane(chip * 2 + my_core)
+        )
+    )
 
     @pl.when(my_core == 1)
     def _():
@@ -261,13 +280,12 @@
         gg_sum[which] = (gg_stage[which, my_core] + gg_pair[which].astype(F32)).astype(BF)
         keep(gg_sum.at[which, my_chip], gg.at[which, my_chip], sem_gg.at[1, which])
 
-        @pl.loop(1, 8)
-        def _(n):
-            chip = chip_to(n)
-            put(
+        each_chip(
+            lambda chip: put(
                 gg_sum.at[which, chip], gg.at[which, my_chip], send_gg.at[1], sem_gg.at[1, which],
                 plane(chip * 2 + my_core),
             )
+        )
 
     wait(qg.at[1], sem_qg.at[1])
 
@@ -332,11 +350,7 @@
                 terms = [ret[named[p][r], r].astype(F32) for r in range(ROUNDS)]
                 tot_stage[p, t] = (terms[0] + terms[1] + terms[2]).astype(BF)
 
-            @pl.loop(1, NP)
-            def _(i):
-                p = plane_to(i)
-                put(tot_stage.at[p, t], dst, send_tot, sem, plane(p))
-
+            each_other(lambda p: put(tot_stage.at[p, t], dst, send_tot, sem, plane(p)))
             keep(tot_stage.at[my_p, t], dst, sem)
 
     def finish(which, out):

time: 87.3 us -> 85.6 us (0.981)
  Pallas kernels: 86.4 us -> 84.7 us
    pallas_call x1, Pallas kernels: 84.4 us -> 82.7 us  [local(): pl.pallas_call(kernel, out_shape=(out,) * 4, in_specs=[smem] * 3 + [hbm]...]
where the time goes in v4:
time: 85.6 us; the launch traced here: 85.3 us
  Pallas kernels  84.7 us (99%)
    pallas_call x1, Pallas kernels, local(): pl.pallas_call(kernel, out_shape=(out,) * 4, in_specs=[smem] * 3 + [hbm]...  82.7 us
    pallas_call x1, Pallas kernels, local(): pl.pallas_call(hand_out, out_shape=(out,) * 4, in_specs=[hbm] * 4, out_sp...  1.98 us

profile of v4, /device:TPU:1, one launch (start us, length us, event | category | flops | bytes accessed | tf_op | source)
XLA Modules:
  0.0 85.3 jit_solution(3428787725854546826)
XLA Ops:
  0.6 82.7 %shard_map.102 = (bf16[128,1024]{1,0:T(8,128)(2,1)}, bf16[128,1024]{1,0:T(8,128)(2,1)}, bf16[128,1024]{1,0:T(8,128)(2,1)}, bf16[128,1024]{1,0:T(8,128)(2,1)}) custom-call(s32[3,128]{1,0:T(4,128)} %matches.1, s32[3]{0:T(128)} %bitcast.1, s32[4]{0:T(128)} %gpos.1, bf16[128,1024]{1,0:T(8,128)(2,1)} %q_in.1, bf16[128,1024]{1,0:T(8,128)(2,1)} %k_in.1, ...), custom_call_target="tpu_custom_call" | custom-call | flops 1700000000 | bytes 2000000 | tf_op jit(solution)/shard_map/pallas_call | solution.py:463
  83.3 2.0 %shard_map.103 = (bf16[128,1024]{1,0:T(8,128)(2,1)}, bf16[128,1024]{1,0:T(8,128)(2,1)}, bf16[128,1024]{1,0:T(8,128)(2,1)}, bf16[128,1024]{1,0:T(8,128)(2,1)}) custom-call(bf16[128,1024]{1,0:T(8,128)(2,1)} %get-tuple-element.8.refs_0_, bf16[128,1024]{1,0:T(8,128)(2,1)} %get-tuple-element.9.refs_1_, bf16[128,1024]{1,0:T(8,128)(2,1)} %get-tuple-element.10.refs_2_, ...), custom_call_target="tpu_custom_call" | custom-call | tf_op jit(solution)/shard_map/pallas_call | solution.py:477

commit v5 on v4

--- a/solution.py
+++ b/solution.py
@@ -9,7 +9,7 @@
 ROUNDS = 3
 NY = 8
 NP = 16
-EARLY = 4
+EARLY = 3
 TOK = 128
 SCALE = HD**-0.5
 LOG2E = 1.4426950408889634
@@ -131,6 +131,13 @@
         def _(y):
             keep(cols(ref, y), moved.at[n, y], sem_moved.at[n])
 
+    wait(moved.at[0], sem_moved.at[0])
+    pl.semaphore_wait(barrier, NY - 1 + NP - 1)
+
+    @pl.loop(1, NY)
+    def _(n):
+        put(moved.at[0, line_to(n)], kv.at[0, my_y], send_kv, sem_kv.at[0, my_y], line(line_to(n)))
+
     row = lax.broadcasted_iota(jnp.int32, (32, TOK), 0)
     lane = lax.broadcasted_iota(jnp.int32, (32, TOK), 1)
     tile = jnp.zeros((32, TOK), F32)
@@ -140,24 +147,14 @@
     for r in range(ROUNDS):
         tile = jnp.where(row == 16 + r, active[r].astype(F32), tile)
     aux[...] = tile.astype(BF)
-    for n in range(4):
+    for n in range(1, 4):
         wait(moved.at[n], sem_moved.at[n])
-
-    pl.semaphore_wait(barrier, NY - 1 + NP - 1)
-
-    @pl.loop(1, NY)
-    def _(n):
-        put(moved.at[0, line_to(n)], kv.at[0, my_y], send_kv, sem_kv.at[0, my_y], line(line_to(n)))
 
     keep(moved.at[0, my_y], kv.at[0, my_y], sem_kv.at[0, my_y])
     keep(moved.at[1, my_y], kv.at[1, my_y], sem_kv.at[1, my_y])
     keep(moved.at[2, my_y], qg.at[0, my_y], sem_qg.at[0])
     keep(moved.at[3, my_y], qg.at[1, my_y], sem_qg.at[1])
     keep(aux, aux_all.at[my_y], sem_aux)
-
-    @pl.loop(1, NY)
-    def _(n):
-        put(aux, aux_all.at[my_y], send_aux, sem_aux, line(line_to(n)))
 
     def hand_on(which, t):
         wait(kv.at[which, t], sem_kv.at[which, t])
@@ -189,6 +186,10 @@
         @pl.when(n > 0)
         def _():
             put(moved.at[1, line_to(n)], kv.at[1, my_y], send_kv, sem_kv.at[1, my_y], line(line_to(n)))
+
+    @pl.loop(1, NY)
+    def _(n):
+        put(aux, aux_all.at[my_y], send_aux, sem_aux, line(line_to(n)))
 
     @pl.loop(0, 4)
     def _(n):
@@ -385,8 +386,8 @@
         send_back(0, turn(n))
 
     share_globals(0, mm(q_t[...], sgrad[...]) * SCALE)
+    finish(1, dv_out)
     give_globals(0)
-    finish(1, dv_out)
 
     @pl.when(my_core == 0)
     def _():

time: 85.6 us -> 84.9 us (level)
  no operation moved by 1% of the time
where the time goes in v5:
time: 84.9 us; the launch traced here: 84.6 us
  Pallas kernels  84 us (99%)
    pallas_call x1, Pallas kernels, local(): pl.pallas_call(kernel, out_shape=(out,) * 4, in_specs=[smem] * 3 + [hbm]...  82 us
    pallas_call x1, Pallas kernels, local(): pl.pallas_call(hand_out, out_shape=(out,) * 4, in_specs=[hbm] * 4, out_sp...  1.98 us

profile of v5, /device:TPU:1, one launch (start us, length us, event | category | flops | bytes accessed | tf_op | source)
XLA Modules:
  0.0 84.6 jit_solution(10011693692116875852)
XLA Ops:
  0.6 82.0 %shard_map.102 = (bf16[128,1024]{1,0:T(8,128)(2,1)}, bf16[128,1024]{1,0:T(8,128)(2,1)}, bf16[128,1024]{1,0:T(8,128)(2,1)}, bf16[128,1024]{1,0:T(8,128)(2,1)}) custom-call(s32[3,128]{1,0:T(4,128)} %matches.1, s32[3]{0:T(128)} %bitcast.1, s32[4]{0:T(128)} %gpos.1, bf16[128,1024]{1,0:T(8,128)(2,1)} %q_in.1, bf16[128,1024]{1,0:T(8,128)(2,1)} %k_in.1, ...), custom_call_target="tpu_custom_call" | custom-call | flops 1700000000 | bytes 2000000 | tf_op jit(solution)/shard_map/pallas_call | solution.py:464
  82.6 2.0 %shard_map.103 = (bf16[128,1024]{1,0:T(8,128)(2,1)}, bf16[128,1024]{1,0:T(8,128)(2,1)}, bf16[128,1024]{1,0:T(8,128)(2,1)}, bf16[128,1024]{1,0:T(8,128)(2,1)}) custom-call(bf16[128,1024]{1,0:T(8,128)(2,1)} %get-tuple-element.8.refs_0_, bf16[128,1024]{1,0:T(8,128)(2,1)} %get-tuple-element.9.refs_1_, bf16[128,1024]{1,0:T(8,128)(2,1)} %get-tuple-element.10.refs_2_, ...), custom_call_target="tpu_custom_call" | custom-call | tf_op jit(solution)/shard_map/pallas_call | solution.py:478

commit v6 on v5

--- a/solution.py
+++ b/solution.py
@@ -156,6 +156,10 @@
     keep(moved.at[3, my_y], qg.at[1, my_y], sem_qg.at[1])
     keep(aux, aux_all.at[my_y], sem_aux)
 
+    @pl.loop(1, NY)
+    def _(n):
+        put(aux, aux_all.at[my_y], send_aux, sem_aux, line(line_to(n)))
+
     def hand_on(which, t):
         wait(kv.at[which, t], sem_kv.at[which, t])
         to_keepers(
@@ -186,10 +190,6 @@
         @pl.when(n > 0)
         def _():
             put(moved.at[1, line_to(n)], kv.at[1, my_y], send_kv, sem_kv.at[1, my_y], line(line_to(n)))
-
-    @pl.loop(1, NY)
-    def _(n):
-        put(aux, aux_all.at[my_y], send_aux, sem_aux, line(line_to(n)))
 
     @pl.loop(0, 4)
     def _(n):

time: 84.9 us -> 85.1 us (level)
  no operation moved by 1% of the time
where the time goes in v6:
time: 85.1 us; the launch traced here: 84.8 us
  Pallas kernels  84.2 us (99%)
    pallas_call x1, Pallas kernels, local(): pl.pallas_call(kernel, out_shape=(out,) * 4, in_specs=[smem] * 3 + [hbm]...  82.2 us
    pallas_call x1, Pallas kernels, local(): pl.pallas_call(hand_out, out_shape=(out,) * 4, in_specs=[hbm] * 4, out_sp...  1.98 us

profile of v6, /device:TPU:1, one launch (start us, length us, event | category | flops | bytes accessed | tf_op | source)
XLA Modules:
  0.0 84.8 jit_solution(13148961327115373991)
XLA Ops:
  0.6 82.2 %shard_map.102 = (bf16[128,1024]{1,0:T(8,128)(2,1)}, bf16[128,1024]{1,0:T(8,128)(2,1)}, bf16[128,1024]{1,0:T(8,128)(2,1)}, bf16[128,1024]{1,0:T(8,128)(2,1)}) custom-call(s32[3,128]{1,0:T(4,128)} %matches.1, s32[3]{0:T(128)} %bitcast.1, s32[4]{0:T(128)} %gpos.1, bf16[128,1024]{1,0:T(8,128)(2,1)} %q_in.1, bf16[128,1024]{1,0:T(8,128)(2,1)} %k_in.1, ...), custom_call_target="tpu_custom_call" | custom-call | flops 1700000000 | bytes 2000000 | tf_op jit(solution)/shard_map/pallas_call | solution.py:464
  82.8 2.0 %shard_map.103 = (bf16[128,1024]{1,0:T(8,128)(2,1)}, bf16[128,1024]{1,0:T(8,128)(2,1)}, bf16[128,1024]{1,0:T(8,128)(2,1)}, bf16[128,1024]{1,0:T(8,128)(2,1)}) custom-call(bf16[128,1024]{1,0:T(8,128)(2,1)} %get-tuple-element.8.refs_0_, bf16[128,1024]{1,0:T(8,128)(2,1)} %get-tuple-element.9.refs_1_, bf16[128,1024]{1,0:T(8,128)(2,1)} %get-tuple-element.10.refs_2_, ...), custom_call_target="tpu_custom_call" | custom-call | tf_op jit(solution)/shard_map/pallas_call | solution.py:478
